TPU v7x, 32 devices: a whole 2x2x4 slice. The times are simulated.
32 devices in a mesh: seq: 8 (over z, core), wsh: 4 (over y, x).
Axes of the slice: x: 2, y: 2, z: 4, core: 2. Of those that a mesh axis runs over, the one named last changes fastest.
Arguments:
- inputs: bfloat16 [2, 4, 1024, 2048], P(None, 'wsh', 'seq'), may hold values from -6 to 6
- segments: int32 [2, 4, 1024], P(None, 'wsh'), may hold values from 0 to 7, never falling along the last dimension, each value on 1 to 256 neighbouring positions
- cotangent: bfloat16 [2, 4, 1024, 2048], P(None, 'wsh', 'seq'), may hold values from -6 to 6
- norm1_gain: bfloat16 [2048], P('wsh'), may hold values from 0.5 to 1.5
- gate_branch_w: bfloat16 [2048, 2560], P('wsh'), may hold values from -0.125 to 0.125
- linear_branch_w: bfloat16 [2048, 2560], P('wsh'), may hold values from -0.125 to 0.125
- conv_weight: bfloat16 [2560, 4], P(('seq', 'wsh')), may hold values from -3 to 3
- input_gate_w: bfloat16 [2560, 160], P(('seq', 'wsh')), may hold values from -0.5 to 0.5
- recur_gate_w: bfloat16 [2560, 160], P(('seq', 'wsh')), may hold values from -0.5 to 0.5
- decay_param: bfloat16 [2560], P(('seq', 'wsh')), may hold values from 5 to 11
- out_proj_w: bfloat16 [2560, 2048], P('wsh'), may hold values from -0.5 to 0.5
- norm2_gain: bfloat16 [2048], P('wsh'), may hold values from 0.5 to 1.5
- mlp_gate_w: bfloat16 [2048, 6144], P('wsh'), may hold values from -0.125 to 0.125
- mlp_up_w: bfloat16 [2048, 6144], P('wsh'), may hold values from -0.125 to 0.125
- mlp_down_w: bfloat16 [6144, 2048], P('wsh'), may hold values from -0.15625 to 0.15625
Outputs:
- block_output: float32 [2, 4, 1024, 2048], P(None, 'wsh', 'seq')
- input_grad: float32 [2, 4, 1024, 2048], P(None, 'wsh', 'seq')
- norm1_gain_grad: float32 [2048], P(('seq', 'wsh'))
- gate_branch_grad: float32 [2048, 2560], P(('seq', 'wsh'))
- linear_branch_grad: float32 [2048, 2560], P(('seq', 'wsh'))
- conv_weight_grad: float32 [2560, 4], P(('seq', 'wsh'))
- input_gate_grad: float32 [2560, 160], P(('seq', 'wsh'))
- recur_gate_grad: float32 [2560, 160], P(('seq', 'wsh'))
- decay_grad: float32 [2560], P(('seq', 'wsh'))
- out_proj_grad: float32 [2560, 2048], P(('seq', 'wsh'))
- norm2_gain_grad: float32 [2048], P(('seq', 'wsh'))
- mlp_gate_grad: float32 [2048, 6144], P(('seq', 'wsh'))
- mlp_up_grad: float32 [2048, 6144], P(('seq', 'wsh'))
- mlp_down_grad: float32 [6144, 2048], P(('seq', 'wsh'))
Inputs may be any that keep to these rules, and one draw needn't show every extreme that they name: `segments`: along each sequence the numbers never fall; every segment holds 1 to 256 positions, and one holds exactly that many.
All inputs are finite; a program needn't handle non-finite values.
Results may differ from a plain program's by a relative error of at most 0.017.
Values may be sent and summed in bfloat16 or wider, within the bound.
No kernel may reach another device: no remote copies, remote signals or barrier semaphores. Data moves between devices by JAX's collectives and lax.ppermute only.
A program may use at most 384 MiB of HBM per device.

v0:
```python
from functools import partial

import jax
import jax.numpy as jnp
from jax import lax
from jax.sharding import PartitionSpec as P

EPS = 1e-06
HIGH = lax.Precision.HIGHEST
span_rows = 128


def as_sent(shard):
    return jax.tree.map(lambda a: a.astype(jnp.bfloat16) if a.dtype == jnp.float32 else a, shard)


def rms_norm(values, gain):
    scale = lax.rsqrt(jnp.mean(values * values, axis=-1, keepdims=True) + EPS)
    return values * scale * gain


def gate_piece(values):
    return jax.nn.gelu(values)


def mlp_piece(gate_pre, up_pre):
    return jax.nn.gelu(gate_pre) * up_pre


def reset_flags(segment_row):
    prior = jnp.concatenate([segment_row[:1] - 1, segment_row[:-1]])
    return (segment_row != prior)[:, None]


def conv_taps(values, weight, segment_row):
    total = values * weight[:, 0]
    for tap in range(1, weight.shape[1]):
        moved = jnp.concatenate(
            [jnp.zeros((tap, values.shape[1]), values.dtype), values[:-tap]], axis=0
        )
        earlier = jnp.concatenate([jnp.full((tap,), -1, jnp.int32), segment_row[:-tap]])
        keep = (earlier == segment_row)[:, None]
        total = total + jnp.where(keep, moved, 0.0) * weight[:, tap]
    return total


def lru_inputs(conv_out, in_gate, rec_gate, decay, reset):
    length, width = conv_out.shape
    block = in_gate.shape[1]
    grouped = conv_out.reshape(length, width // block, block)
    gate_in = jax.nn.sigmoid(
        jnp.einsum(
            "thi,hij->thj", grouped, in_gate.reshape(width // block, block, block), precision=HIGH
        ).reshape(length, width)
    )
    gate_rec = jax.nn.sigmoid(
        jnp.einsum(
            "thi,hij->thj", grouped, rec_gate.reshape(width // block, block, block), precision=HIGH
        ).reshape(length, width)
    )
    log_decay = -8.0 * gate_rec * jax.nn.softplus(-decay)
    scale = jnp.where(reset, 1.0, jnp.sqrt(-jnp.expm1(2.0 * log_decay)))
    return (log_decay, scale * gate_in * conv_out)


def blocked_recurrence(log_decay, driven, segment_row):
    length, width = log_decay.shape
    span = min(span_rows, length)
    count = length // span
    block_ends = segment_row[span - 1 :: span]
    before = jnp.concatenate([jnp.full((1,), -1, jnp.int32), block_ends[:-1]])
    offsets = jnp.arange(span)
    lower = offsets[:, None] >= offsets[None, :]
    lower_ones = lower.astype(jnp.float32)

    @jax.checkpoint
    def advance(state, items):
        decay_rows, drive_rows, seg_rows, seg_before = items
        cumulative = jnp.dot(lower_ones, decay_rows, precision=HIGH)
        same = ((seg_rows[:, None] == seg_rows[None, :]) & lower).astype(jnp.float32)
        inner = jnp.exp(cumulative) * jnp.dot(
            same, jnp.exp(-cumulative) * drive_rows, precision=HIGH
        )
        carried = (
            jnp.where((seg_rows == seg_before)[:, None], jnp.exp(cumulative), 0.0) * state[None, :]
        )
        states = inner + carried
        return (states[-1], states)

    start = jnp.zeros((width,), jnp.float32)
    _, states = lax.scan(
        advance,
        start,
        (
            log_decay.reshape(count, span, width),
            driven.reshape(count, span, width),
            segment_row.reshape(count, span),
            before,
        ),
    )
    return states.reshape(length, width)


def mixer(values, in_gate, rec_gate, conv_w, decay, segment_row):
    reset = reset_flags(segment_row)
    conv_out = conv_taps(values, conv_w, segment_row)
    log_decay, driven = lru_inputs(conv_out, in_gate, rec_gate, decay, reset)
    return blocked_recurrence(log_decay, driven, segment_row)


def scatter_ffn(terms):
    return lax.psum_scatter(terms, ("seq", "wsh"), scatter_dimension=0, tiled=True)


def scatter_branch(terms):
    return lax.psum_scatter(terms, ("seq", "wsh"), scatter_dimension=0, tiled=True)


def scatter_mixer(terms):
    return jax.tree.map(
        lambda part: part.astype(jnp.float32),
        lax.psum_scatter(as_sent(terms), "wsh", scatter_dimension=0, tiled=True),
    )


def accumulate(total, item):
    return item if total is None else jax.tree.map(jnp.add, total, item)


def per_device(
    inputs,
    segments,
    cotangent,
    norm1_gain,
    gate_branch_w,
    linear_branch_w,
    conv_weight,
    input_gate_w,
    recur_gate_w,
    decay_param,
    out_proj_w,
    norm2_gain,
    mlp_gate_w,
    mlp_up_w,
    mlp_down_w,
):
    f32 = jnp.float32
    bf16 = jnp.bfloat16
    micro = inputs.shape[0]
    ffn_total = None
    branch_total = None
    mixer_total = None
    outputs = []
    input_grads = []
    for index in range(micro):
        front = (
            lax.all_gather(norm1_gain, "wsh", axis=0, tiled=True),
            lax.all_gather(gate_branch_w, "wsh", axis=0, tiled=True),
            lax.all_gather(linear_branch_w, "wsh", axis=0, tiled=True),
            lax.all_gather(conv_weight, "wsh", axis=0, tiled=True),
            lax.all_gather(input_gate_w, "wsh", axis=0, tiled=True),
            lax.all_gather(recur_gate_w, "wsh", axis=0, tiled=True),
            lax.all_gather(decay_param, "wsh", axis=0, tiled=True),
        )
        gain_one, w_gate, w_linear, conv_w, in_gate, rec_gate, decay = front
        segment_row = segments[index, 0]
        x_rows = inputs[index, 0].astype(f32)
        normed, norm_one_back = jax.vjp(rms_norm, x_rows, gain_one.astype(f32))
        normed_low = normed.astype(bf16)
        gate_pre = jnp.dot(normed_low, w_gate, preferred_element_type=f32)
        linear_pre = jnp.dot(normed_low, w_linear, preferred_element_type=f32)
        gate, gate_back = jax.vjp(gate_piece, gate_pre)
        sent = lax.all_to_all(
            linear_pre.astype(bf16), "seq", split_axis=1, concat_axis=0, tiled=True
        )
        mixed, mixer_back = jax.vjp(
            partial(mixer, segment_row=segment_row),
            sent.astype(f32),
            in_gate.astype(f32),
            rec_gate.astype(f32),
            conv_w.astype(f32),
            decay.astype(f32),
        )
        returned = lax.all_to_all(
            mixed.astype(bf16), "seq", split_axis=0, concat_axis=1, tiled=True
        )
        returned_f = returned.astype(f32)
        product_low = (gate * returned_f).astype(bf16)
        back_part = (
            lax.all_gather(out_proj_w, "wsh", axis=0, tiled=True),
            lax.all_gather(norm2_gain, "wsh", axis=0, tiled=True),
            lax.all_gather(mlp_gate_w, "wsh", axis=0, tiled=True),
            lax.all_gather(mlp_up_w, "wsh", axis=0, tiled=True),
            lax.all_gather(mlp_down_w, "wsh", axis=0, tiled=True),
        )
        w_out, gain_two, mlp_gate, mlp_up, mlp_down = back_part
        hidden = x_rows + jnp.dot(product_low, w_out, preferred_element_type=f32)
        normed_two, norm_two_back = jax.vjp(rms_norm, hidden, gain_two.astype(f32))
        normed_two_low = normed_two.astype(bf16)
        up_gate = jnp.dot(normed_two_low, mlp_gate, preferred_element_type=f32)
        up_lin = jnp.dot(normed_two_low, mlp_up, preferred_element_type=f32)
        active, mlp_back = jax.vjp(mlp_piece, up_gate, up_lin)
        active_low = active.astype(bf16)
        outputs.append(hidden + jnp.dot(active_low, mlp_down, preferred_element_type=f32))
        grad_rows = cotangent[index, 0]
        grad_down = jnp.einsum("tf,td->fd", active_low, grad_rows, preferred_element_type=f32)
        grad_active = jnp.einsum("td,fd->tf", grad_rows, mlp_down, preferred_element_type=f32)
        grad_gate_pre, grad_up_pre = mlp_back(grad_active)
        grad_gate_low = grad_gate_pre.astype(bf16)
        grad_up_low = grad_up_pre.astype(bf16)
        grad_mlp_gate = jnp.einsum(
            "td,tf->df", normed_two_low, grad_gate_low, preferred_element_type=f32
        )
        grad_mlp_up = jnp.einsum(
            "td,tf->df", normed_two_low, grad_up_low, preferred_element_type=f32
        )
        grad_normed_two = jnp.einsum(
            "tf,df->td", grad_gate_low, mlp_gate, preferred_element_type=f32
        ) + jnp.einsum("tf,df->td", grad_up_low, mlp_up, preferred_element_type=f32)
        grad_hidden_norm, grad_gain_two = norm_two_back(grad_normed_two)
        grad_hidden = grad_rows.astype(f32) + grad_hidden_norm
        grad_branch = grad_hidden.astype(bf16)
        grad_out = jnp.einsum("tr,td->rd", product_low, grad_branch, preferred_element_type=f32)
        grad_product = jnp.einsum("td,rd->tr", grad_branch, w_out, preferred_element_type=f32)
        ffn_terms = (grad_out, grad_gain_two, grad_mlp_gate, grad_mlp_up, grad_down)
        ffn_total = accumulate(ffn_total, ffn_terms)
        grad_gate = grad_product * returned_f
        grad_mixed = (grad_product * gate).astype(bf16)
        grad_channels = lax.all_to_all(grad_mixed, "seq", split_axis=1, concat_axis=0, tiled=True)
        grad_sent, grad_in_gate, grad_rec_gate, grad_conv, grad_decay = mixer_back(
            grad_channels.astype(f32)
        )
        mixer_terms = (grad_conv, grad_in_gate, grad_rec_gate, grad_decay)
        mixer_total = accumulate(mixer_total, mixer_terms)
        grad_linear = lax.all_to_all(
            grad_sent.astype(bf16), "seq", split_axis=0, concat_axis=1, tiled=True
        )
        (grad_gate_pre_one,) = gate_back(grad_gate)
        grad_gate_one = grad_gate_pre_one.astype(bf16)
        grad_w_gate = jnp.einsum("td,tr->dr", normed_low, grad_gate_one, preferred_element_type=f32)
        grad_w_linear = jnp.einsum("td,tr->dr", normed_low, grad_linear, preferred_element_type=f32)
        grad_normed = jnp.einsum(
            "tr,dr->td", grad_gate_one, w_gate, preferred_element_type=f32
        ) + jnp.einsum("tr,dr->td", grad_linear, w_linear, preferred_element_type=f32)
        grad_x_norm, grad_gain_one = norm_one_back(grad_normed)
        input_grads.append(grad_hidden + grad_x_norm)
        branch_terms = (grad_gain_one, grad_w_gate, grad_w_linear)
        branch_total = accumulate(branch_total, branch_terms)
    ffn_total = scatter_ffn(ffn_total)
    mixer_total = scatter_mixer(mixer_total)
    branch_total = scatter_branch(branch_total)
    sum_out, sum_gain_two, sum_mlp_gate, sum_mlp_up, sum_down = ffn_total
    sum_conv, sum_in_gate, sum_rec_gate, sum_decay = mixer_total
    sum_gain_one, sum_gate, sum_linear = branch_total
    return (
        jnp.stack(outputs)[:, None],
        jnp.stack(input_grads)[:, None],
        sum_gain_one,
        sum_gate,
        sum_linear,
        sum_conv,
        sum_in_gate,
        sum_rec_gate,
        sum_decay,
        sum_out,
        sum_gain_two,
        sum_mlp_gate,
        sum_mlp_up,
        sum_down,
    )


def solution(mesh):
    placed = (
        P(None, "wsh", "seq", None),
        P(None, "wsh", None),
        P(None, "wsh", "seq", None),
        P("wsh"),
        P("wsh", None),
        P("wsh", None),
        P(("seq", "wsh"), None),
        P(("seq", "wsh"), None),
        P(("seq", "wsh"), None),
        P(("seq", "wsh")),
        P("wsh", None),
        P("wsh"),
        P("wsh", None),
        P("wsh", None),
        P("wsh", None),
    )
    return jax.shard_map(
        per_device,
        mesh=mesh,
        in_specs=placed,
        out_specs=(
            P(None, "wsh", "seq", None),
            P(None, "wsh", "seq", None),
            P(("seq", "wsh")),
            P(("seq", "wsh"), None),
            P(("seq", "wsh"), None),
            P(("seq", "wsh"), None),
            P(("seq", "wsh"), None),
            P(("seq", "wsh"), None),
            P(("seq", "wsh")),
            P(("seq", "wsh"), None),
            P(("seq", "wsh")),
            P(("seq", "wsh"), None),
            P(("seq", "wsh"), None),
            P(("seq", "wsh"), None),
        ),
        check_vma=False,
    )
```

profile of v0, /device:TPU:0, one launch (start us, length us, event | category | flops | bytes accessed | tf_op | source)
XLA Modules:
  0.0 4116.2 jit_solution(11717389463730630794)
XLA Ops:
  14.1 9.5 all-gather
  45.1 72.6 %all-gather.12.cloned.1.call-done = bf16[2048,2560]{1,0:T(8,128)(2,1)} async-done(((bf16[512,2560]{1,0:T(8,128)(2,1)}), bf16[2048,2560]{1,0:T(8,128)(2,1)}) %all-gather.12.cloned.1.call-update) | async-done | bytes 10485776 | tf_op jit(solution)/shard_map/all_gather | solution.py:159
  129.1 10.0 all_gather.52
  161.5 17.2 all-to-all-done.2
  201.4 38.8 while.71
  247.0 31.5 while.70
  311.9 22.4 all-gather.14.cloned.1.call-done
  340.2 9.5 multiply_convert_fusion.6
  352.5 211.3 %all-gather.16.cloned.1.call-done = bf16[2048,6144]{1,0:T(8,128)(2,1)} async-done(((bf16[512,6144]{1,0:T(8,128)(2,1)}), bf16[2048,6144]{1,0:T(8,128)(2,1)}) %all-gather.16.cloned.1.call-update) | async-done | bytes 25165840 | tf_op jit(solution)/shard_map/all_gather | solution.py:192
  563.8 13.9 fusion.240
  577.7 215.6 %all-gather.18.cloned.1.call-done = bf16[2048,6144]{1,0:T(8,128)(2,1)} async-done(((bf16[512,6144]{1,0:T(8,128)(2,1)}), bf16[2048,6144]{1,0:T(8,128)(2,1)}) %all-gather.18.cloned.1.call-update) | async-done | bytes 25165840 | tf_op jit(solution)/shard_map/all_gather | solution.py:193
  793.3 14.1 fusion.241
  807.3 215.4 %all-gather.20.cloned.1.call-done = bf16[6144,2048]{1,0:T(8,128)(2,1)} async-done(((bf16[1536,2048]{1,0:T(8,128)(2,1)}), bf16[6144,2048]{1,0:T(8,128)(2,1)}) %all-gather.20.cloned.1.call-update) | async-done | bytes 25165840 | tf_op jit(solution)/shard_map/all_gather | solution.py:194
  1022.7 17.3 multiply_convert_fusion.1
  1040.1 14.3 fusion.244
  1054.4 15.4 multiply_reduce_fusion.11
  1069.8 10.2 fusion.242
  1080.0 10.3 fusion.243
  1090.3 15.3 multiply_convert_fusion
  1105.7 14.3 fusion.247
  1120.0 15.7 multiply_reduce_fusion.10
  1139.2 9.5 multiply_convert_fusion.4
  1154.3 10.0 multiply_convert_fusion.5
  1182.9 95.5 %while.73 = (s32[]{:T(128)}, f32[320]{0:T(512)S(1)}, f32[8,128,320]{1,0,2:T(8,128)}, f32[8,128,320]{1,2,0:T(8,128)S(1)}, f32[8,320]{1,0:T(8,128)}, /*index=5*/f3...) while((s32[]{:T(128)}, f32[320]{0:T(512)S(1)}, ...), condition=%wide.region_16.18_spmd.clone, body=%wide.region_14.17_spmd.clone.sunk | while | flops 252657472 | bytes 4191801 | solution.py:91
  1283.5 100.7 %while.72 = (s32[]{:T(128)}, f32[320]{0:T(512)S(1)}, f32[8,128,320]{1,0,2:T(8,128)}, f32[8,128,320]{1,2,0:T(8,128)}, f32[8,320]{1,0:T(8,128)}, /*index=5*/f32[8,...) while((s32[]{:T(128)}, f32[320]{0:T(512)S(1)}, ...), condition=%wide.region_11.13_spmd.clone, body=%wide.region_9.12_spmd.clone.sunk | while | flops 252657472 | bytes 4191801 | solution.py:91
  1401.3 13.6 convolution_add_fusion.5
  1416.1 9.8 fusion.207
  1425.9 14.0 convolution_add_fusion.3
  1472.6 15.6 all-to-all-done.5
  1501.3 12.2 all-to-all-done.7
  1513.5 14.0 convolution_add_fusion.4
  1528.5 21.0 fusion.252
  1549.5 32.6 convolution_add_fusion.1
  1582.2 21.2 fusion.253
  1603.4 32.5 convolution_add_fusion
  1637.1 21.3 fusion.192
  1658.5 32.5 convolution_add_fusion.2
  1695.0 10.3 fusion.90
  1705.3 10.6 fusion.91
  1734.6 14.8 all-reduce.32
  1761.3 9.3 fusion.167
  1770.6 39.8 all-reduce.31
  1815.2 81.3 %reduce-scatter.10.cloned.1.call-done = f32[64,2560]{1,0:T(8,128)} async-done(((f32[2048,2560]{1,0:T(8,128)}), f32[64,2560]{1,0:T(8,128)}) %reduce-scatter.10.cloned.1.call-update) | async-done | bytes 655376 | tf_op jit(solution)/shard_map/reduce_scatter | solution.py:116
  1896.5 449.7 %reduce-scatter.18.cloned.1.call-done = f32[80,2048]{1,0:T(8,128)} async-done(((f32[2560,2048]{1,0:T(8,128)}), f32[80,2048]{1,0:T(8,128)}) %reduce-scatter.18.cloned.1.call-update) | async-done | bytes 655376 | tf_op jit(solution)/shard_map/reduce_scatter | solution.py:112
  2346.2 449.0 %reduce-scatter.12.cloned.1.call-done = f32[64,2560]{1,0:T(8,128)} async-done(((f32[2048,2560]{1,0:T(8,128)}), f32[64,2560]{1,0:T(8,128)}) %reduce-scatter.12.cloned.1.call-update) | async-done | bytes 655376 | tf_op jit(solution)/shard_map/reduce_scatter | solution.py:116
  2795.2 439.2 %reduce-scatter.20.cloned.1.call-done = f32[64,6144]{1,0:T(8,128)} async-done(((f32[2048,6144]{1,0:T(8,128)}), f32[64,6144]{1,0:T(8,128)}) %reduce-scatter.20.cloned.1.call-update) | async-done | bytes 1572880 | tf_op jit(solution)/shard_map/reduce_scatter | solution.py:112
  3234.3 437.6 %reduce-scatter.22.cloned.1.call-done = f32[64,6144]{1,0:T(8,128)} async-done(((f32[2048,6144]{1,0:T(8,128)}), f32[64,6144]{1,0:T(8,128)}) %reduce-scatter.22.cloned.1.call-update) | async-done | bytes 1572880 | tf_op jit(solution)/shard_map/reduce_scatter | solution.py:112
  3672.0 437.6 %reduce-scatter.24.cloned.1.call-done = f32[192,2048]{1,0:T(8,128)} async-done(((f32[6144,2048]{1,0:T(8,128)}), f32[192,2048]{1,0:T(8,128)}) %reduce-scatter.24.cloned.1.call-update) | async-done | bytes 1572880 | tf_op jit(solution)/shard_map/reduce_scatter | solution.py:112
  (832 shorter events, 532.9 us)
Async XLA Ops:
  7.2 110.6 %all-gather.12.cloned.1.call-start = ((), (), s32[]{:S(2)}) async-start(), calls=%async_computation.17 | async-start | bytes 13107200 | tf_op jit(solution)/shard_map/all_gather | solution.py:159
  7.9 296.8 %all-gather.10.cloned.1.call-start = ((), (), s32[]{:S(2)}) async-start(), calls=%async_computation.16 | async-start | bytes 13107200 | tf_op jit(solution)/shard_map/all_gather | solution.py:158
  8.7 325.7 %all-gather.14.cloned.1.call-start = ((), (), s32[]{:S(2)}) async-start(), calls=%async_computation.18 | async-start | bytes 13107200 | tf_op jit(solution)/shard_map/all_gather | solution.py:190
  9.4 554.4 %all-gather.16.cloned.1.call-start = ((), (), s32[]{:S(2)}) async-start(), calls=%async_computation.19 | async-start | bytes 31457280 | tf_op jit(solution)/shard_map/all_gather | solution.py:192
  10.0 783.3 %all-gather.18.cloned.1.call-start = ((), (), s32[]{:S(2)}) async-start(), calls=%async_computation.20 | async-start | bytes 31457280 | tf_op jit(solution)/shard_map/all_gather | solution.py:193
  10.6 1012.2 %all-gather.20.cloned.1.call-start = ((), (), s32[]{:S(2)}) async-start(), calls=%async_computation.21 | async-start | bytes 31457280 | tf_op jit(solution)/shard_map/all_gather | solution.py:194
  23.6 1489.9 %copy-start.79 = (f32[4,1,512]{2,1,0:T(1,128)}, f32[4,1,512]{2,1,0:T(1,128)S(1)}, u32[]{:S(2)}) copy-start(f32[4,1,512]{2,1,0:T(1,128)S(1)} %convert_element_type.313) | copy-start | bytes 24580
  44.5 115.9 %copy-start.135 = (bf16[320]{0:T(512)(128)(2,1)}, bf16[320]{0:T(512)(128)(2,1)S(1)}, u32[]{:S(2)}) copy-start(bf16[320]{0:T(512)(128)(2,1)S(1)} %all-reduce.26) | copy-start | bytes 1924
  44.7 135.2 %copy-start.105 = (f32[320]{0:T(512)}, f32[320]{0:T(512)S(1)}, u32[]{:S(2)}) copy-start(f32[320]{0:T(512)S(1)} %get-tuple-element.964) | copy-start | bytes 3844
  44.8 135.2 %copy-start.111 = (f32[320]{0:T(512)}, f32[320]{0:T(512)S(1)}, u32[]{:S(2)}) copy-start(f32[320]{0:T(512)S(1)} %get-tuple-element.965) | copy-start | bytes 3844
  44.8 135.2 %copy-start.113 = (f32[320]{0:T(512)}, f32[320]{0:T(512)S(1)}, u32[]{:S(2)}) copy-start(f32[320]{0:T(512)S(1)} %get-tuple-element.966) | copy-start | bytes 3844
  44.8 135.2 %copy-start.115 = (f32[320]{0:T(512)}, f32[320]{0:T(512)S(1)}, u32[]{:S(2)}) copy-start(f32[320]{0:T(512)S(1)} %get-tuple-element.967) | copy-start | bytes 3844
  45.1 78.3 %copy-start.144 = (f32[128]{0:T(128)}, f32[128]{0:T(128)S(1)}, u32[]{:S(2)}) copy-start(f32[128]{0:T(128)S(1)} %get-tuple-element.962) | copy-start | bytes 1540
  45.1 78.3 %copy-start.146 = (f32[128]{0:T(128)}, f32[128]{0:T(128)S(1)}, u32[]{:S(2)}) copy-start(f32[128]{0:T(128)S(1)} %get-tuple-element.963) | copy-start | bytes 1540
  45.1 1447.0 %copy-start.107 = (f32[128]{0:T(128)}, f32[128]{0:T(128)S(1)}, u32[]{:S(2)}) copy-start(f32[128]{0:T(128)S(1)} %fusion.217) | copy-start | bytes 1540
  45.1 295.0 %copy-start.100 = (f32[128]{0:T(128)}, f32[128]{0:T(128)S(1)}, u32[]{:S(2)}) copy-start(f32[128]{0:T(128)S(1)} %fusion.219) | copy-start | bytes 1540
  124.4 30.7 all-to-all-start
  139.0 47.0 %copy-start.87 = (bf16[320,160]{1,0:T(8,128)(2,1)}, bf16[320,160]{1,0:T(8,128)(2,1)S(1)}, u32[]{:S(2)}) copy-start(bf16[320,160]{1,0:T(8,128)(2,1)S(1)} %all_gather.52) | copy-start | bytes 307204
  147.8 46.4 %copy-start.85 = (bf16[320,160]{1,0:T(8,128)(2,1)}, bf16[320,160]{1,0:T(8,128)(2,1)S(1)}, u32[]{:S(2)}) copy-start(bf16[320,160]{1,0:T(8,128)(2,1)S(1)} %all_gather.54) | copy-start | bytes 307204
  155.1 23.6 all-to-all-start.2
  161.1 34.5 copy-start.92
  161.2 34.4 copy-start.117
  161.3 34.4 copy-start.119
  240.3 38.3 all-to-all-start.3
  278.6 23.4 all-to-all-start.1
  340.1 795.6 %copy-start.13 = (f32[128,2048]{1,0:T(8,128)}, f32[128,2048]{1,0:T(8,128)S(1)}, u32[]{:S(2)}) copy-start(f32[128,2048]{1,0:T(8,128)S(1)} %get-tuple-element.1141) | copy-start | bytes 3145732
  351.4 784.4 %copy-start.15 = (f32[128,2048]{1,0:T(8,128)}, f32[128,2048]{1,0:T(8,128)S(1)}, u32[]{:S(2)}) copy-start(f32[128,2048]{1,0:T(8,128)S(1)} %get-tuple-element.1143) | copy-start | bytes 3145732
  1149.7 25.6 all-to-all-start.6
  1175.3 103.1 %all-to-all-start.4 = ((bf16[128,8,320]{0,2,1:T(8,128)(2,1)}), bf16[128,8,320]{0,2,1:T(8,128)(2,1)}, u32[]{:S(2)}, u32[]{:S(2)}) async-start(bf16[128,8,320]{0,2,1:T(8,128)(2,1)} %bitcast.44), calls=%async_computation.4 | async-start | bytes 1310720 | tf_op jit(solution)/shard_map/all_to_all | solution.py:229
  1180.4 570.2 %reduce-scatter.14.cloned.1.call-start = ((), (), s32[]{:S(2)}) async-start(), calls=%async_computation.24 | async-start | bytes 204800 | tf_op jit(solution)/shard_map/reduce_scatter | solution.py:122
  1283.5 100.7 %copy-start.8 = (f32[1024,320]{0,1:T(8,128)S(1)}, f32[1024,320]{0,1:T(8,128)}, u32[]{:S(2)}) copy-start(f32[1024,320]{0,1:T(8,128)} %copy-done.6) | copy-start | bytes 3932164
  1283.5 100.7 %copy-start.93 = (f32[320]{0:T(512)S(1)}, f32[320]{0:T(512)}, u32[]{:S(2)}) copy-start(f32[320]{0:T(512)} %copy-done.92) | copy-start | bytes 3844
  1283.5 100.7 %copy-start.118 = (pred[1024]{0:T(1024)(128)(4,1)S(1)}, pred[1024]{0:T(1024)(128)(4,1)}, u32[]{:S(2)}) copy-start(pred[1024]{0:T(1024)(128)(4,1)} %copy-done.117) | copy-start | bytes 3076
  1283.5 100.7 %copy-start.120 = (pred[1024]{0:T(1024)(128)(4,1)S(1)}, pred[1024]{0:T(1024)(128)(4,1)}, u32[]{:S(2)}) copy-start(pred[1024]{0:T(1024)(128)(4,1)} %copy-done.119) | copy-start | bytes 3076
  1283.5 100.7 %copy-start.143 = (f32[320]{0:T(512)S(1)}, f32[320]{0:T(512)}, u32[]{:S(2)}) copy-start(f32[320]{0:T(512)} %get-tuple-element.1132) | copy-start | bytes 3844
  1395.9 356.2 %reduce-scatter.16.cloned.1.call-start = ((), (), s32[]{:S(2)}) async-start(), calls=%async_computation.25 | async-start | bytes 204800 | tf_op jit(solution)/shard_map/reduce_scatter | solution.py:122
  1401.2 495.3 %reduce-scatter.10.cloned.1.call-start = ((), (), s32[]{:S(2)}) async-start(), calls=%async_computation.22 | async-start | bytes 21626880 | tf_op jit(solution)/shard_map/reduce_scatter | solution.py:116
  1414.9 931.3 %reduce-scatter.18.cloned.1.call-start = ((), (), s32[]{:S(2)}) async-start(), calls=%async_computation.26 | async-start | bytes 21626880 | tf_op jit(solution)/shard_map/reduce_scatter | solution.py:112
  1461.9 26.3 all-to-all-start.5
  1488.2 25.3 all-to-all-start.7
  1492.1 1303.1 %reduce-scatter.12.cloned.1.call-start = ((), (), s32[]{:S(2)}) async-start(), calls=%async_computation.23 | async-start | bytes 21626880 | tf_op jit(solution)/shard_map/reduce_scatter | solution.py:116
  1527.5 1706.8 %reduce-scatter.20.cloned.1.call-start = ((), (), s32[]{:S(2)}) async-start(), calls=%async_computation.27 | async-start | bytes 51904512 | tf_op jit(solution)/shard_map/reduce_scatter | solution.py:112
  1582.2 2089.8 %reduce-scatter.22.cloned.1.call-start = ((), (), s32[]{:S(2)}) async-start(), calls=%async_computation.28 | async-start | bytes 51904512 | tf_op jit(solution)/shard_map/reduce_scatter | solution.py:112
  1635.9 2473.6 %reduce-scatter.24.cloned.1.call-start = ((), (), s32[]{:S(2)}) async-start(), calls=%async_computation.29 | async-start | bytes 51904512 | tf_op jit(solution)/shard_map/reduce_scatter | solution.py:112
  1761.3 50.2 %copy-start.145 = (f32[128]{0:T(128)S(1)}, f32[128]{0:T(128)}, u32[]{:S(2)}) copy-start(f32[128]{0:T(128)} %copy-done.144) | copy-start | bytes 1540
  1761.3 50.2 %copy-start.147 = (f32[128]{0:T(128)S(1)}, f32[128]{0:T(128)}, u32[]{:S(2)}) copy-start(f32[128]{0:T(128)} %copy-done.146) | copy-start | bytes 1540
  1761.3 50.2 %copy-start.59 = (f32[128,2048]{1,0:T(8,128)S(1)}, f32[128,2048]{1,0:T(8,128)}, u32[]{:S(2)}) copy-start(f32[128,2048]{1,0:T(8,128)} %copy-done.57) | copy-start | bytes 3145732
  1761.3 50.2 %copy-start.62 = (f32[128,2048]{1,0:T(8,128)S(1)}, f32[128,2048]{1,0:T(8,128)}, u32[]{:S(2)}) copy-start(f32[128,2048]{1,0:T(8,128)} %get-tuple-element.1094) | copy-start | bytes 3145732
  (138 other events, 945.5 us)
Sparse Core Ops, SparseCore 0:
  9.9 107.8 all-gather.11
  119.6 107.6 all-gather.9
  229.2 105.1 all-gather.13
  336.1 227.7 all-gather.15
  565.5 227.6 all-gather.17
  795.0 227.7 all-gather.19
  1396.0 24.3 reduce-scatter.13
  1423.2 23.9 reduce-scatter.15
  1450.0 446.4 reduce-scatter.9
  1899.2 446.9 reduce-scatter.17
  2349.1 446.0 reduce-scatter.11
  2802.0 432.2 reduce-scatter.19
  3241.3 430.5 reduce-scatter.21
  3678.8 430.7 reduce-scatter.23
where the time goes:
time: 4130 us; the launch traced here: 4120 us
  waiting for transfers between devices  3090 us (75%)
  matrix products  562 us (14%)
  local copies, waits for them, and re-layouts  219 us (5%)
  blocking collectives  109 us (3%)
  other arithmetic  82.6 us (2%)
    reduce_scatter x4, waiting for transfers between devices, scatter_ffn(): lax.psum_scatter(terms, ('seq', 'wsh'), scatter_dimension=0, tiled=True)  1760 us
    reduce_scatter x2, waiting for transfers between devices, scatter_branch(): lax.psum_scatter(terms, ('seq', 'wsh'), scatter_dimension=0, tiled=True)  530 us
    all_gather x1, waiting for transfers between devices, per_device(): lax.all_gather(mlp_up_w, 'wsh', axis=0, tiled=True)  216 us
    all_gather x1, waiting for transfers between devices, per_device(): lax.all_gather(mlp_down_w, 'wsh', axis=0, tiled=True)  215 us
    all_gather x1, waiting for transfers between devices, per_device(): lax.all_gather(mlp_gate_w, 'wsh', axis=0, tiled=True)  211 us
    dynamic_update_slice x32, local copies, waits for them, and re-layouts, blocked_recurrence(): lax.scan(advance, start, (log_decay.reshape(count, span, width), driven.r...  91.2 us
  transfers between devices with their start and end apart: 22, of which 15 were waited for; matrix products, arithmetic and copies ran while one was open for 15% of the time, Pallas kernels for 0%

commit v1 on v0

v1 whole, which is shorter than its diff:
```python
from functools import partial

import jax
import jax.numpy as jnp
from jax import lax
from jax.experimental import pallas as pl
from jax.experimental.pallas import tpu as pltpu
from jax.sharding import PartitionSpec as P

EPS = 1e-06
AXES = ("seq", "wsh")
LANES = 128
VMEM_LIMIT = 48 * 1024 * 1024
f32 = jnp.float32
bf16 = jnp.bfloat16


def gelu_parts(v):
    k = 0.7978845608028654
    t = jnp.tanh(k * (v + 0.044715 * v * v * v))
    half = 0.5 * (1.0 + t)
    slope = half + 0.5 * v * (1.0 - t * t) * k * (1.0 + 3.0 * 0.044715 * v * v)
    return v * half, slope


def lru_parts(zr, soft):
    rg = jax.nn.sigmoid(zr)
    la = -8.0 * rg * soft
    a = jnp.exp(la)
    x = 2.0 * la
    series = -x * (
        1.0
        + x
        * (
            1.0 / 2.0
            + x
            * (
                1.0 / 6.0
                + x
                * (
                    1.0 / 24.0
                    + x * (1.0 / 120.0 + x * (1.0 / 720.0 + x * (1.0 / 5040.0 + x * (1.0 / 40320.0))))
                )
            )
        )
    )
    rest = jnp.where(x > -0.5, series, 1.0 - a * a)
    return rg, a, rest


def conv_kernel(T, Q, taps, pre_ref, halo_ref, mask_ref, w_ref, conv_ref):
    w = [w_ref[k : k + 1, :] for k in range(taps)]
    past = tuple(halo_ref[pl.ds((taps - 2 - k) * Q, Q), :] for k in range(taps - 1))

    def step(t, past):
        u = pre_ref[pl.ds(t, Q, stride=T), :].astype(bf16).astype(f32)
        row = pl.multiple_of(t * Q, Q)
        depth = mask_ref[pl.ds(row, Q), :]
        total = w[0] * u
        for k in range(1, taps):
            total = total + jnp.where(depth >= k, past[k - 1], 0.0) * w[k]
        conv_ref[pl.ds(row, Q), :] = total
        return (u,) + past[:-1]

    lax.fori_loop(0, T, step, past, unroll=8)


def scan_kernel(T, Q, zi_ref, zr_ref, conv_ref, mask_ref, soft_ref, h_ref, a_ref, end_ref):
    soft = soft_ref[0:1, :]

    def step(t, carry):
        h, prod = carry
        rows = pl.ds(pl.multiple_of(t * Q, Q), Q)
        keep = mask_ref[rows, :] >= 1.0
        ig = jax.nn.sigmoid(zi_ref[rows, :])
        _, a, rest = lru_parts(zr_ref[rows, :], soft)
        mult = jnp.where(keep, jnp.sqrt(rest), 1.0)
        a = jnp.where(keep, a, 0.0)
        h = a * h + mult * ig * conv_ref[rows, :]
        prod = prod * a
        h_ref[rows, :] = h
        a_ref[rows, :] = a
        return h, prod

    zero = jnp.zeros((Q, h_ref.shape[1]), f32)
    h, prod = lax.fori_loop(0, T, step, (zero, zero + 1.0), unroll=8)
    end_ref[0:Q, :] = h
    end_ref[Q : 2 * Q, :] = prod


def carry_kernel(T, Q, h_ref, a_ref, carry_ref, ypre_ref, state_ref, hs_ref, prod_ref, tmp_ref):
    def step(t, carried):
        rows = pl.ds(pl.multiple_of(t * Q, Q), Q)
        carried = carried * a_ref[rows, :]
        h = h_ref[rows, :] + carried
        state_ref[rows, :] = h
        tmp_ref[pl.ds(t, Q, stride=T), :] = h
        return carried

    lax.fori_loop(0, T, step, carry_ref[...], unroll=8)

    def block(i, _):
        rows = pl.ds(pl.multiple_of(i * 64, 64), 64)
        hs = tmp_ref[rows, :].astype(bf16)
        hs_ref[rows, :] = hs
        gate, _ = gelu_parts(ypre_ref[rows, :])
        prod_ref[rows, :] = (gate * hs.astype(f32)).astype(bf16)
        return 0

    lax.fori_loop(0, T * Q // 64, block, 0)


def back_scan_kernel(T, Q, dprod_ref, ypre_ref, hs_ref, a_ref, dy_ref, e_ref, first_ref, tmp_ref):
    def block(i, _):
        rows = pl.ds(pl.multiple_of(i * 64, 64), 64)
        dprod = dprod_ref[rows, :]
        gate, slope = gelu_parts(ypre_ref[rows, :])
        dy_ref[rows, :] = (dprod * hs_ref[rows, :].astype(f32) * slope).astype(bf16)
        tmp_ref[rows, :] = (dprod * gate).astype(bf16).astype(f32)
        return 0

    lax.fori_loop(0, T * Q // 64, block, 0)

    def step(i, moved):
        t = T - 1 - i
        rows = pl.ds(pl.multiple_of(t * Q, Q), Q)
        e = tmp_ref[pl.ds(t, Q, stride=T), :] + moved
        e_ref[rows, :] = e
        return e * a_ref[rows, :]

    zero = jnp.zeros((Q, e_ref.shape[1]), f32)
    first_ref[...] = lax.fori_loop(0, T, step, zero, unroll=8)


def back_gates_kernel(
    T,
    Q,
    e_ref,
    right_ref,
    zi_ref,
    zr_ref,
    conv_ref,
    state_ref,
    carry_ref,
    mask_ref,
    soft_ref,
    dzi_ref,
    dzr_ref,
    dconv_ref,
    ddecay_ref,
    tmpi_ref,
    tmpr_ref,
):
    soft = soft_ref[0:1, :]
    sig = soft_ref[1:2, :]

    def one(t, moved, total, prior):
        rows = pl.ds(pl.multiple_of(t * Q, Q), Q)
        keep = mask_ref[rows, :] >= 1.0
        e = e_ref[rows, :] + moved
        ig = jax.nn.sigmoid(zi_ref[rows, :])
        rg, a, rest = lru_parts(zr_ref[rows, :], soft)
        conv = conv_ref[rows, :]
        mult = jnp.where(keep, jnp.sqrt(rest), 1.0)
        dla = jnp.where(keep, e * a * prior - e * ig * conv * (a * a) / mult, 0.0)
        total = total + dla * rg
        tmpr_ref[rows, :] = dla * (-8.0 * soft) * rg * (1.0 - rg)
        em = e * mult
        tmpi_ref[rows, :] = em * conv * ig * (1.0 - ig)
        dconv_ref[rows, :] = em * ig
        return moved * jnp.where(keep, a, 0.0), total

    def step(i, carry):
        moved, total = carry
        t = T - 1 - i
        prior = state_ref[pl.ds(pl.multiple_of((t - 1) * Q, Q), Q), :]
        return one(t, moved, total, prior)

    zero = jnp.zeros((Q, e_ref.shape[1]), f32)
    moved, total = lax.fori_loop(0, T - 1, step, (right_ref[...], zero), unroll=4)
    _, total = one(0, moved, total, carry_ref[...])
    ddecay_ref[...] = 8.0 * sig * jnp.sum(total, axis=0, keepdims=True)

    def block(i, _):
        rows = pl.ds(pl.multiple_of(i * 64, 64), 64)
        dzi_ref[rows, :] = tmpi_ref[rows, :].astype(bf16)
        dzr_ref[rows, :] = tmpr_ref[rows, :].astype(bf16)
        return 0

    lax.fori_loop(0, T * Q // 64, block, 0)


def back_conv_kernel(
    T, Q, taps, dconv_ref, next_ref, pre_ref, halo_ref, mask_ref, w_ref, dus_ref, dw_ref, tmp_ref
):
    w = [w_ref[k : k + 1, :] for k in range(taps)]
    past = tuple(halo_ref[pl.ds((taps - 2 - k) * Q, Q), :] for k in range(taps - 1))
    zero = jnp.zeros((Q, pre_ref.shape[1]), f32)

    def terms(dconv, depth):
        return tuple(jnp.where(depth >= k, dconv, 0.0) for k in range(1, taps))

    def step(t, carry):
        past, waiting, sums = carry
        u = pre_ref[pl.ds(t, Q, stride=T), :].astype(bf16).astype(f32)
        rows = pl.ds(pl.multiple_of(t * Q, Q), Q)
        dconv = dconv_ref[rows, :]
        masked = terms(dconv, mask_ref[rows, :])
        done = waiting[taps - 2] + w[taps - 1] * masked[taps - 2]
        older = [w[0] * dconv]
        for k in range(1, taps - 1):
            older.append(waiting[k - 1] + w[k] * masked[k - 1])
        sums = (sums[0] + dconv * u,) + tuple(
            sums[k] + masked[k - 1] * past[k - 1] for k in range(1, taps)
        )

        @pl.when(t >= taps - 1)
        def _():
            tmp_ref[pl.ds(t - (taps - 1), Q, stride=T), :] = done

        return (u,) + past[:-1], tuple(older), sums

    start = (past, (zero,) * (taps - 1), (zero,) * taps)
    _, waiting, sums = lax.fori_loop(0, T, step, start, unroll=4)
    for j in range(taps - 1):
        rows = pl.ds(j * Q, Q)
        masked = terms(next_ref[rows, :], mask_ref[pl.ds((T + j) * Q, Q), :])
        done = waiting[taps - 2] + w[taps - 1] * masked[taps - 2]
        older = [zero]
        for k in range(1, taps - 1):
            older.append(waiting[k - 1] + w[k] * masked[k - 1])
        tmp_ref[pl.ds(T + j - (taps - 1), Q, stride=T), :] = done
        waiting = tuple(older)
    for k in range(taps):
        dw_ref[k : k + 1, :] = jnp.sum(sums[k], axis=0, keepdims=True)

    def block(i, _):
        rows = pl.ds(pl.multiple_of(i * 64, 64), 64)
        dus_ref[rows, :] = tmp_ref[rows, :].astype(bf16)
        return 0

    lax.fori_loop(0, T * Q // 64, block, 0)


def tiled_call(kernel, ins, outs, scratch=()):
    channels = outs[0][0][1]

    def spec(shape, first):
        return pl.BlockSpec((shape[0], LANES), (lambda c: (0, 0)) if first is None else (lambda c: (0, c + first)))

    moved = sum(a.size * a.dtype.itemsize for a, _ in ins)
    moved += sum(shape[0] * shape[1] * jnp.dtype(kind).itemsize for shape, kind in outs)
    work = outs[0][0][0] * channels
    return pl.pallas_call(
        kernel,
        grid=(pl.cdiv(channels, LANES),),
        in_specs=[spec(a.shape, first) for a, first in ins],
        out_specs=[spec(shape, 0) for shape, _ in outs],
        out_shape=[jax.ShapeDtypeStruct(shape, kind) for shape, kind in outs],
        scratch_shapes=[pltpu.VMEM((rows, LANES), f32) for rows in scratch],
        compiler_params=pltpu.CompilerParams(vmem_limit_bytes=VMEM_LIMIT),
        cost_estimate=pl.CostEstimate(flops=40 * work, bytes_accessed=moved, transcendentals=4 * work),
    )(*[a for a, _ in ins])


def assemble(places, blocks, rows_total, part, count, weights):
    columns = blocks[0].shape[1] // weights
    copies_total = ((len(blocks) - 1) * count + 1) * weights

    def kernel(places_ref, *refs):
        sources, outs, sems = refs[: len(blocks)], refs[len(blocks) : -1], refs[-1]
        copies = []

        def put(ref, start, rows, i):
            at = pl.multiple_of(places_ref[i], 16)
            for k, out in enumerate(outs):
                source = ref.at[pl.ds(start, rows), pl.ds(k * columns, columns)]
                copy = pltpu.make_async_copy(source, out.at[pl.ds(at, rows), :], sems.at[len(copies)])
                copy.start()
                copies.append(copy)

        i = 0
        for ref in sources[:-1]:
            for j in range(count):
                put(ref, j * part, part, i)
                i += 1
        put(sources[-1], 0, sources[-1].shape[0], i)
        for copy in copies:
            copy.wait()

    return pl.pallas_call(
        kernel,
        in_specs=[pl.BlockSpec(memory_space=pltpu.SMEM)] + [pl.BlockSpec(memory_space=pl.ANY)] * len(blocks),
        out_specs=[pl.BlockSpec(memory_space=pltpu.VMEM)] * weights,
        out_shape=[jax.ShapeDtypeStruct((rows_total, columns), blocks[0].dtype)] * weights,
        scratch_shapes=[pltpu.SemaphoreType.DMA((copies_total,))],
        compiler_params=pltpu.CompilerParams(vmem_limit_bytes=VMEM_LIMIT),
        cost_estimate=pl.CostEstimate(
            flops=0, bytes_accessed=4 * rows_total * columns * weights, transcendentals=0
        ),
    )(places, *blocks)


def norm_rows(pieces, gain, rows):
    width = pieces[0].shape[1]
    step = 16

    def kernel(gain_ref, *refs):
        out_ref = refs[-1]
        for i, ref in enumerate(refs[:-1]):

            @pl.when(pl.program_id(0) == i)
            def _():
                def body(k, _):
                    at = pl.ds(pl.multiple_of(k * step, step), step)
                    v = ref[at, :].astype(f32)
                    scale = lax.rsqrt(jnp.mean(v * v, axis=-1, keepdims=True) + EPS)
                    out_ref[at, :] = (v * scale * gain_ref[0:1, :]).astype(bf16)
                    return 0

                lax.fori_loop(0, rows // step, body, 0)

    return pl.pallas_call(
        kernel,
        grid=(len(pieces),),
        in_specs=[pl.BlockSpec((8, width), lambda i: (0, 0))]
        + [pl.BlockSpec(p.shape, lambda i: (0, 0)) for p in pieces],
        out_specs=pl.BlockSpec((rows, width), lambda i: (i, 0)),
        out_shape=jax.ShapeDtypeStruct((rows * len(pieces), width), bf16),
        compiler_params=pltpu.CompilerParams(vmem_limit_bytes=VMEM_LIMIT),
        cost_estimate=pl.CostEstimate(
            flops=6 * rows * len(pieces) * width,
            bytes_accessed=4 * rows * len(pieces) * width,
            transcendentals=0,
        ),
    )(jnp.broadcast_to(gain[None, :], (8, width)), *pieces)


def after(value, *others):
    return lax.optimization_barrier((value,) + others)[0]


def per_device(
    seqs,
    wide,
    inputs,
    segments,
    cotangent,
    norm1_gain,
    gate_branch_w,
    linear_branch_w,
    conv_weight,
    input_gate_w,
    recur_gate_w,
    decay_param,
    out_proj_w,
    norm2_gain,
    mlp_gate_w,
    mlp_up_w,
    mlp_down_w,
):
    micro, _, T, D = inputs.shape
    length = segments.shape[2]
    Q = micro * wide
    chips = seqs // 2
    C = gate_branch_w.shape[1] // wide
    tiles = pl.cdiv(C, LANES)
    wide_C = tiles * LANES
    F = mlp_gate_w.shape[1] // wide
    block = input_gate_w.shape[1]
    taps = conv_weight.shape[1]
    own = micro * T
    shard = D // wide
    seq = lax.axis_index("seq")
    wsh = lax.axis_index("wsh")
    chip, core = seq // 2, seq % 2

    def perm_of(move_seq, flip=0):
        pairs = [(s, move_seq(s), w) for s in range(seqs) for w in range(wide)]
        return [(s * wide + w, d * wide + (w ^ flip)) for s, d, w in pairs if 0 <= d < seqs]

    def along_wsh(flip):
        return perm_of(lambda s: s, flip)

    def along_seq(shift):
        return perm_of(lambda s: s + shift)

    twin_perm = perm_of(lambda s: s ^ 1)
    pair_perm = perm_of(lambda s: s ^ 2)
    ring_perm = perm_of(lambda s: (s + 2) % seqs)
    from_owner = [(k // wide * wide + k % wide, k % seqs * wide + k // seqs) for k in range(seqs * wide)]
    halves_to_owner = []
    for w in range(wide):
        for s in range(seqs):
            halves_to_owner.append((s * wide + w, w * seqs + s % 2 * chips + s // 2))

    def send(value, perm):
        return lax.ppermute(value, AXES, perm)

    def spread(piece):
        return [piece] + [send(piece, along_wsh(r)) for r in range(1, wide)]

    def collect(products):
        got = [send(products[r].astype(bf16), along_wsh(r)) for r in range(wide - 1, 0, -1)]
        total = products[0]
        for value in got:
            total = total + value.astype(f32)
        return total

    def token_rows(value, r):
        return value[r * own : (r + 1) * own]

    def own_columns(weights, r, start, rows):
        parts = []
        for weight in weights:
            columns = weight.shape[1] // wide
            value = lax.dynamic_slice(weight, (start, (wsh ^ r) * columns), (rows, columns))
            parts.append(jnp.pad(value, ((0, 0), (0, -columns % LANES))))
        return jnp.concatenate(parts, axis=1)

    def fetch(weights, rows, at):
        got = [send(own_columns(weights, r, at * rows, rows), along_wsh(r)) for r in range(wide - 1, 0, -1)]
        return jnp.concatenate(got[::-1], axis=0)

    def place(weights, fetched, rows):
        places = [(wsh ^ r) * shard + at * rows for _, at in fetched for r in range(1, wide)]
        places = jnp.stack(places + [wsh * shard]).astype(jnp.int32)
        blocks = [value for value, _ in fetched] + [own_columns(weights, 0, 0, shard)]
        out = assemble(places, blocks, D, rows, wide - 1, len(weights))
        return [value[:, : w.shape[1] // wide] for value, w in zip(out, weights)]

    def pair_sums(terms):
        pairs = []
        for k in list(range(1, chips)) + [0]:
            target = lax.rem(chip - k + chips, chips)
            other = send(terms(target, 1 - core).astype(bf16), twin_perm)
            pairs.append((terms(target, core) + other.astype(f32)).astype(bf16))
        return list(lax.optimization_barrier(tuple(pairs)))

    def ring_step(held, pair):
        return send(held.astype(bf16), ring_perm).astype(f32) + pair.astype(f32)

    def ring_sum(pairs):
        held = pairs[0]
        for pair in pairs[1:]:
            held = ring_step(held, pair)
        return held

    def strided_terms(left, right):
        n = left.shape[1] // seqs

        def terms(target, half):
            return t_dot(lax.dynamic_slice(left, (0, (2 * target + half) * n), (left.shape[0], n)), right)

        return terms

    def halved_terms(left, right):
        n = left.shape[1] // seqs

        def terms(target, half):
            return t_dot(lax.dynamic_slice(left, (0, (half * chips + target) * n), (left.shape[0], n)), right)

        return terms

    def columns_to_rows(value, weights, gain):
        rows = value.shape[0]
        weight_rows = [lax.dynamic_slice(w, (seq * rows, 0), (rows, w.shape[1])) for w in weights]
        weight_rows = jnp.concatenate(weight_rows, axis=1).astype(f32)
        own_gain = lax.dynamic_slice(gain, (seq * rows,), (rows,))
        term = jnp.sum(value * weight_rows, axis=1) / own_gain
        low = value.astype(bf16).reshape(rows, 2, -1)
        term_low = term.astype(bf16)
        rest = (term - term_low.astype(f32)).astype(bf16)
        extra = jnp.pad(jnp.stack([term_low, rest], axis=1)[:, :, None], ((0, 0), (0, 0), (0, LANES - 1)))
        n = low.shape[2]
        low = jnp.concatenate([low, extra], axis=2)
        got = lax.all_to_all(low, "wsh", split_axis=0, concat_axis=2, tiled=True).astype(f32)
        got = got.reshape(rows // wide, 2, wide, n + LANES)
        grads = got[:, :, :, :n].reshape(rows // wide, 2, wide * n)
        return grads[:, 0], grads[:, 1], jnp.sum(got[:, :, :, n], axis=(1, 2))

    def dot(a, b):
        return jnp.dot(a, b, preferred_element_type=f32)

    def dot_t(a, b):
        return lax.dot_general(a, b, (((1,), (1,)), ((), ())), preferred_element_type=f32)

    def t_dot(a, b):
        return lax.dot_general(a, b, (((0,), (0,)), ((), ())), preferred_element_type=f32)

    def scale_of(v):
        return lax.rsqrt(jnp.mean(v * v, axis=-1, keepdims=True) + EPS)

    def norm_back(dn, v, gain):
        s = scale_of(v)
        scaled = dn * gain
        return s * scaled - v * (s * s * s) * jnp.mean(scaled * v, axis=-1, keepdims=True)

    branch = [gate_branch_w, linear_branch_w]
    branch_rows = shard // 4
    held = fetch(branch, branch_rows, seq % 4)
    paired = send(held, pair_perm)
    here, there = seq % 4, seq % 4 ^ 2
    branch_parts = [
        (held, here),
        (paired, there),
        (send(held, twin_perm), here ^ 1),
        (send(paired, twin_perm), there ^ 1),
    ]
    w_gate, w_linear = place(branch, branch_parts, branch_rows)

    rows = jnp.pad(segments[:, 0], ((0, 0), (taps - 1, taps - 1)), constant_values=-1)
    whole_depth = jnp.zeros((micro, length + taps - 1), f32)
    for k in range(1, taps):
        same = rows[:, taps - 1 :] == rows[:, taps - 1 - k : rows.shape[1] - k]
        same = same & (jnp.arange(length + taps - 1) >= k)[None, :]
        whole_depth = whole_depth + same.astype(f32)
    depth = lax.dynamic_slice(whole_depth, (0, seq * T), (micro, T + taps - 1)).astype(bf16)

    note = jnp.zeros((16, D), bf16)
    note = note.at[:micro, : T + taps - 1].set(depth)
    note = note.at[micro, :shard].set(norm1_gain)
    note = note.at[micro + 1, :shard].set(norm2_gain)
    noted = jnp.concatenate([inputs[:, 0].reshape(own, D), note], axis=0)
    x_pieces = spread(after(noted, held))
    notes = [piece[own:] for piece in x_pieces]
    depth = jnp.concatenate([n[:micro, : T + taps - 1] for n in notes], axis=0).astype(f32)
    mask = jnp.broadcast_to(depth.T[:, :, None], (T + taps - 1, Q, LANES)).reshape(-1, LANES)
    mask_own = mask[: T * Q]

    def joined(k):
        whole = jnp.zeros((D,), bf16)
        for r in range(wide):
            whole = lax.dynamic_update_slice(whole, notes[r][micro + k, :shard], ((wsh ^ r) * shard,))
        return whole.astype(f32)

    gain_one, gain_two = joined(0), joined(1)
    small = jnp.concatenate([input_gate_w, recur_gate_w, conv_weight, decay_param[:, None]], axis=1)
    pad = -small.shape[1] % LANES
    small = send(jnp.pad(small, ((0, 0), (0, pad))), from_owner)
    small = lax.all_gather(small, "seq", axis=0, tiled=True)
    in_gate = small[:, :block]
    rec_gate = small[:, block : 2 * block]
    conv_w = small[:, 2 * block : 2 * block + taps].astype(f32).T
    conv_w = jnp.pad(conv_w, ((0, 8 - taps), (0, 0)))
    decay = small[:, 2 * block + taps].astype(f32)
    soft = jnp.stack([jax.nn.softplus(-decay), jax.nn.sigmoid(-decay)])
    soft = jnp.pad(soft, ((0, 6), (0, 0)))
    blocks = C // block
    eye = jnp.eye(blocks, dtype=bf16)

    def dense(gate_w):
        spread_w = gate_w.reshape(blocks, block, 1, block) * eye[:, None, :, None]
        return jnp.pad(spread_w.reshape(C, C), ((0, 0), (0, wide_C - C)))

    gates_w = jnp.concatenate([dense(in_gate), dense(rec_gate)], axis=1)

    xn = norm_rows(x_pieces, gain_one, own)
    last = xn.reshape(Q, T, D)[:, T - (taps - 1) :].transpose(1, 0, 2).reshape((taps - 1) * Q, D)
    halo = send(dot(last, w_linear).astype(bf16), along_seq(1)).astype(f32)
    us_pre = dot(xn, w_linear)

    mlp = [mlp_gate_w, mlp_up_w]
    mlp_rows = shard // seqs
    held = fetch([after(w, *x_pieces[1:]) for w in mlp], mlp_rows, seq)
    mlp_parts = []
    for k in range(chips):
        if k:
            held = send(held, ring_perm)
        source = lax.rem(chip - k + chips, chips) * 2
        mlp_parts.append((held, source + core))
        mlp_parts.append((send(held, twin_perm), source + 1 - core))

    (conv,) = tiled_call(
        partial(conv_kernel, T, Q, taps),
        [(us_pre, 0), (halo, 0), (mask_own, None), (conv_w, 0)],
        [((T * Q, C), f32)],
    )
    conv_low = conv.astype(bf16)
    z = dot(conv_low, gates_w)
    h_local, a, end = tiled_call(
        partial(scan_kernel, T, Q),
        [(z, 0), (z, tiles), (conv, 0), (mask_own, None), (soft, 0)],
        [((T * Q, C), f32), ((T * Q, C), f32), ((2 * Q, C), f32)],
    )
    reach = pl.cdiv(length // 4, T)
    ends = [send(end, along_seq(k)) for k in range(1, reach + 1)]
    ypre = dot(after(xn, end), w_gate)
    carry, through = ends[0][:Q], ends[0][Q:]
    for value in ends[1:]:
        carry = carry + through * value[:Q]
        through = through * value[Q:]
    state, hs, prod = tiled_call(
        partial(carry_kernel, T, Q),
        [(h_local, 0), (a, 0), (carry, 0), (ypre, 0)],
        [((T * Q, C), f32), ((T * Q, C), bf16), ((T * Q, C), bf16)],
        [T * Q],
    )
    following_ends = [send(end[Q:], along_seq(-k)) for k in range(1, reach)]

    x_own = inputs[:, 0].reshape(own, D).astype(f32)
    hidden = x_own + collect([dot(token_rows(prod, r), out_proj_w) for r in range(wide)])
    hn_own = (hidden * scale_of(hidden) * gain_two).astype(bf16)
    hn_pieces = spread(hn_own)
    hn = jnp.concatenate(hn_pieces, axis=0)
    w_gate2, w_up = place(mlp, mlp_parts, mlp_rows)
    g_pieces = spread(after(cotangent[:, 0].reshape(own, D), *hn_pieces[1:]))
    gpre = dot(hn, w_gate2)
    uppre = dot(hn, w_up)
    act_gate, act_slope = gelu_parts(gpre)
    act = (act_gate * uppre).astype(bf16)

    g_group = jnp.concatenate(g_pieces, axis=0)
    g_own = cotangent[:, 0].reshape(own, D).astype(f32)
    dact = dot_t(g_group, mlp_down_w)
    dgp = (dact * uppre * act_slope).astype(bf16)
    dup = (dact * act_gate).astype(bf16)
    products = [dot_t(token_rows(dgp, r), w_gate2) + dot_t(token_rows(dup, r), w_up) for r in range(wide)]
    products = [products[0]] + [p.astype(bf16) for p in products[1:]]
    dhn = collect(products)
    down_pairs = pair_sums(halved_terms(after(act, *products[1:]), g_group))
    mlp_pairs = pair_sums(strided_terms(after(hn, *products[1:]), jnp.concatenate([dgp, dup], axis=1)))
    down_sum = ring_sum(down_pairs)
    mlp_sum = ring_sum([after(mlp_pairs[0], down_sum)] + mlp_pairs[1:])
    dh1 = g_own + norm_back(dhn, hidden, gain_two)

    do_own = dh1.astype(bf16)
    do_pieces = spread(do_own)
    do = jnp.concatenate(do_pieces, axis=0)
    act_late = after(act, *do_pieces[1:])
    block_output = hidden + collect([dot(token_rows(act_late, r), mlp_down_w) for r in range(wide)])
    dprod = dot_t(do, out_proj_w)
    dy, e_local, first = tiled_call(
        partial(back_scan_kernel, T, Q),
        [(dprod, 0), (ypre, 0), (hs, 0), (a, 0)],
        [((T * Q, C), bf16), ((T * Q, C), f32), ((Q, C), f32)],
        [T * Q],
    )
    firsts = [send(first, along_seq(-k)) for k in range(1, reach + 1)]
    out_pairs = pair_sums(halved_terms(after(prod, first), do))
    right, through = firsts[0], None
    for value, past in zip(firsts[1:], following_ends):
        through = past if through is None else through * past
        right = right + through * value
    dzi, dzr, dconv_direct, ddecay = tiled_call(
        partial(back_gates_kernel, T, Q),
        [
            (e_local, 0),
            (right, 0),
            (z, 0),
            (z, tiles),
            (conv, 0),
            (state, 0),
            (carry, 0),
            (mask_own, None),
            (soft, 0),
        ],
        [((T * Q, C), bf16), ((T * Q, C), bf16), ((T * Q, C), f32), ((1, C), f32)],
        [T * Q, T * Q],
    )
    dconv = dconv_direct + dot_t(dzi, gates_w[:, :C]) + dot_t(dzr, gates_w[:, wide_C : wide_C + C])
    following = send(dconv[: (taps - 1) * Q].astype(bf16), along_seq(-1)).astype(f32)
    dus, dconv_w = tiled_call(
        partial(back_conv_kernel, T, Q, taps),
        [(dconv, 0), (following, 0), (us_pre, 0), (halo, 0), (mask, None), (conv_w, 0)],
        [((T * Q, C), bf16), ((8, C), f32)],
        [T * Q],
    )

    products = [dot_t(token_rows(dy, r), w_gate) + dot_t(token_rows(dus, r), w_linear) for r in range(wide)]
    products = [products[0]] + [p.astype(bf16) for p in products[1:]]
    dxn = collect(products)
    branch_pairs = pair_sums(strided_terms(after(xn, *products[1:]), jnp.concatenate([dy, dus], axis=1)))
    out_sum = ring_sum([after(out_pairs[0], mlp_sum)] + out_pairs[1:])
    branch_sum = ring_sum(branch_pairs)

    def diagonal(terms):
        return jnp.concatenate(
            [terms[b * block : (b + 1) * block, b * block : (b + 1) * block] for b in range(blocks)], axis=0
        )

    late_low = after(conv_low, *products[1:])
    small_terms = jnp.concatenate(
        [
            diagonal(t_dot(late_low, dzi)),
            diagonal(t_dot(late_low, dzr)),
            dconv_w[:taps].T,
            ddecay.T,
            jnp.zeros((C, pad), f32),
        ],
        axis=1,
    )

    def small_chunk(target, half):
        n = C // seqs
        return lax.dynamic_slice(small_terms, ((half * chips + target) * n, 0), (n, small_terms.shape[1]))

    small_sum = ring_sum(pair_sums(small_chunk))
    input_grad = dh1 + norm_back(dxn, x_own, gain_one)

    def owned(value):
        return send(value.astype(bf16), halves_to_owner).astype(f32)

    small_grad = owned(small_sum)
    gate2_grad, up_grad, gain_two_grad = columns_to_rows(mlp_sum, [w_gate2, w_up], gain_two)
    gate_grad, linear_grad, gain_one_grad = columns_to_rows(branch_sum, [w_gate, w_linear], gain_one)
    return (
        block_output.reshape(inputs.shape),
        input_grad.reshape(inputs.shape),
        gain_one_grad,
        gate_grad,
        linear_grad,
        small_grad[:, 2 * block : 2 * block + taps],
        small_grad[:, :block],
        small_grad[:, block : 2 * block],
        small_grad[:, 2 * block + taps],
        owned(out_sum),
        gain_two_grad,
        gate2_grad,
        up_grad,
        owned(down_sum),
    )


def solution(mesh):
    both = ("seq", "wsh")
    tokens = P(None, "wsh", "seq", None)
    return jax.shard_map(
        partial(per_device, mesh.shape["seq"], mesh.shape["wsh"]),
        mesh=mesh,
        in_specs=(
            tokens,
            P(None, "wsh", None),
            tokens,
            P("wsh"),
            P("wsh", None),
            P("wsh", None),
            P(both, None),
            P(both, None),
            P(both, None),
            P(both),
            P("wsh", None),
            P("wsh"),
            P("wsh", None),
            P("wsh", None),
            P("wsh", None),
        ),
        out_specs=(
            tokens,
            tokens,
            P(both),
            P(both, None),
            P(both, None),
            P(both, None),
            P(both, None),
            P(both, None),
            P(both),
            P(both, None),
            P(both),
            P(both, None),
            P(both, None),
            P(both, None),
        ),
        check_vma=False,
    )
```

time: 4130 us -> 1030 us (0.25)
  the two profiles are of different devices: /device:TPU:0 before, /device:TPU:26 now
where the time goes in v1:
time: 1030 us; the launch traced here: 1020 us
  waiting for transfers between devices  308 us (30%)
  matrix products  231 us (22%)
  starting transfers between devices  217 us (21%)
  local copies, waits for them, and re-layouts  105 us (10%)
  Pallas kernels  76.2 us (7%)
  other arithmetic  62.5 us (6%)
  blocking collectives  16.4 us (2%)
    ppermute x86, waiting for transfers between devices, send(): return lax.ppermute(value, AXES, perm)  308 us
    ppermute x86, starting transfers between devices, send(): return lax.ppermute(value, AXES, perm)  165 us
    dot_general x34, matrix products, t_dot(): lax.dot_general(a, b, (((0,), (0,)), ((), ())), preferred_element_type=f32)  91.4 us
    dot_general x14, matrix products, dot(): return jnp.dot(a, b, preferred_element_type=f32)  79 us
    dot_general x20, matrix products, dot_t(): lax.dot_general(a, b, (((1,), (1,)), ((), ())), preferred_element_type=f32)  60.2 us
    all_to_all x2, starting transfers between devices, columns_to_rows(): lax.all_to_all(low, 'wsh', split_axis=0, concat_axis=2, tiled=True)  52.1 us
    pallas_call x6, Pallas kernels, tiled_call(): pl.pallas_call(kernel, grid=(pl.cdiv(channels, LANES),), in_specs=[spec(a...  50.6 us
    unnamed x207, local copies, waits for them, and re-layouts  26.9 us
  transfers between devices with their start and end apart: 88, of which 26 were waited for; matrix products, arithmetic and copies ran while one was open for 30% of the time, Pallas kernels for 7%

profile of v1, /device:TPU:26, one launch (start us, length us, event | category | flops | bytes accessed | tf_op | source)
XLA Modules:
  0.0 1019.5 jit_solution(1316299898480738538)
XLA Ops:
  18.4 16.4 %all_gather.3 = bf16[640,384]{1,0:T(8,128)(2,1)S(1)} all-gather(bf16[80,384]{1,0:T(8,128)(2,1)S(1)} %collective-permute-done.10), channel_id=1, replica_groups=mesh['seq'=8,'wsh'=4] {'seq'}, dimensions={0}, use_global_device_ids=true | all-gather | bytes 552960 | tf_op jit(solution)/shard_map/all_gather | solution.py:541
  58.0 9.5 collective-permute-done.6.refs_1_
  67.6 23.1 %collective-permute-done.4.refs_2_ = bf16[272,2048]{1,0:T(8,128)(2,1)} collective-permute-done((bf16[272,2048]{1,0:T(8,128)(2,1)}, bf16[272,2048]{1,0:T(8,128)(2,1)}, u32[]{:S(2)}, u32[]{:S(2)}) %collective-permute-start.4) | collective-permute-done | bytes 1114144 | tf_op jit(solution)/shard_map/ppermute | solution.py:398
  109.2 10.3 %shard_map.254 = bf16[1024,2048]{1,0:T(8,128)(2,1)} custom-call(f32[8,2048]{1,0:T(8,128)S(1)} %broadcast_in_dim.18.gain_ref, bf16[272,2048]{1,0:T(8,128)(2,1)S(1)} %copy-done.12, bf16[272,2048]{1,0:T(8,128)(2,1)} %collective-permute-done.3.refs_1_, bf16[272,2048]{1,0:T(8,128)(2,1)} %collective-permute-done.4.refs_2_, ...), custom_call_target="tpu_custom_call" | custom-call | flops 12582912 | bytes 8388608 | tf_op jit(solution)/shard_map/pallas_call | solution.py:323
  125.9 5.5 shard_map.255
  139.4 10.6 %collective-permute-done.9 = bf16[24,640]{1,0:T(8,128)(2,1)S(1)} collective-permute-done((bf16[24,640]{1,0:T(8,128)(2,1)S(1)}, bf16[24,640]{1,0:T(8,128)(2,1)S(1)}, u32[]{:S(2)}, u32[]{:S(2)}) %collective-permute-start.9) | collective-permute-done | bytes 30752 | tf_op jit(solution)/shard_map/ppermute | solution.py:398
  160.7 7.9 shard_map.257
  171.9 7.1 fusion.190.ypre_ref
  179.1 6.9 shard_map.258
  199.4 20.4 %collective-permute-done.13 = bf16[256,2048]{1,0:T(8,128)(2,1)} collective-permute-done((bf16[256,2048]{1,0:T(8,128)(2,1)}, bf16[256,2048]{1,0:T(8,128)(2,1)}, u32[]{:S(2)}, u32[]{:S(2)}) %collective-permute-start.13) | collective-permute-done | bytes 1048608 | tf_op jit(solution)/shard_map/ppermute | solution.py:398
  219.8 18.0 %collective-permute-done.14 = bf16[256,2048]{1,0:T(8,128)(2,1)} collective-permute-done((bf16[256,2048]{1,0:T(8,128)(2,1)}, bf16[256,2048]{1,0:T(8,128)(2,1)}, u32[]{:S(2)}, u32[]{:S(2)}) %collective-permute-start.14) | collective-permute-done | bytes 1048608 | tf_op jit(solution)/shard_map/ppermute | solution.py:398
  252.7 6.1 collective-permute-start.27
  258.8 11.7 %collective-permute-done.16 = bf16[256,2048]{1,0:T(8,128)(2,1)} collective-permute-done((bf16[256,2048]{1,0:T(8,128)(2,1)}, bf16[256,2048]{1,0:T(8,128)(2,1)}, u32[]{:S(2)}, u32[]{:S(2)}) %collective-permute-start.16) | collective-permute-done | bytes 1048608 | tf_op jit(solution)/shard_map/ppermute | solution.py:398
  270.5 21.8 %collective-permute-done.17 = bf16[256,2048]{1,0:T(8,128)(2,1)} collective-permute-done((bf16[256,2048]{1,0:T(8,128)(2,1)}, bf16[256,2048]{1,0:T(8,128)(2,1)}, u32[]{:S(2)}, u32[]{:S(2)}) %collective-permute-start.17) | collective-permute-done | bytes 1048608 | tf_op jit(solution)/shard_map/ppermute | solution.py:398
  307.3 11.5 %collective-permute-done.29 = bf16[256,2048]{1,0:T(8,128)(2,1)} collective-permute-done((bf16[256,2048]{1,0:T(8,128)(2,1)}, bf16[256,2048]{1,0:T(8,128)(2,1)}, u32[]{:S(2)}, u32[]{:S(2)}) %collective-permute-start.29) | collective-permute-done | bytes 1048608 | tf_op jit(solution)/shard_map/ppermute | solution.py:398
  320.7 23.4 %collective-permute-done.30 = bf16[256,2048]{1,0:T(8,128)(2,1)S(1)} collective-permute-done((bf16[256,2048]{1,0:T(8,128)(2,1)}, bf16[256,2048]{1,0:T(8,128)(2,1)S(1)}, u32[]{:S(2)}, u32[]{:S(2)}) %collective-permute-start.30) | collective-permute-done | bytes 1048608 | tf_op jit(solution)/shard_map/ppermute | solution.py:398
  344.2 8.6 fusion.191
  354.9 9.7 shard_map.259
  364.6 13.0 %fusion.178 = f32[1024,1536]{1,0:T(8,128)} fusion(bf16[2048,1536]{1,0:T(8,128)(2,1)} %get-tuple-element.113, bf16[256,2048]{1,0:T(8,128)(2,1)} %collective-permute-done.18, bf16[256,2048]{1,0:T(8,128)(2,1)} %collective-permute-done.17, bf16[256,2048]{1,0:T(8,128)(2,1)} %collective-permute-done.16, bf16[256,2048]{1,0:T(8,128)(2,1)} %multiply_convert_fusion.2), kind=kOutput, calls=%fused_computation.351 | convolution fusion | flops 6459228160 | bytes 16777216 | tf_op jit(solution)/shard_map/dot_general | solution.py:483
  377.7 19.7 %fusion.6 = (bf16[1024,1536]{1,0:T(8,128)(2,1)}, bf16[1024,1536]{1,0:T(8,128)(2,1)}, bf16[1024,1536]{1,0:T(8,128)(2,1)}) fusion(f32[1024,1536]{1,0:T(8,128)} %fusion.191, f32[1024,1536]{1,0:T(8,128)} %fusion.178, bf16[2048,1536]{1,0:T(8,128)(2,1)} %get-tuple-element.112, bf16[256,2048]{1,0:T(8,128)(2,1)} %collective-permute-done.18, ...), kind=kOutput, calls=%fused_computation.9 | convolution fusion | flops 6498549760 | bytes 32505856 | tf_op jit(solution)/shard_map/dot_general | solution.py:483
  397.4 6.3 fusion.54
  430.9 6.1 convolution_convert_fusion
  437.0 5.8 convolution_convert_fusion.1
  442.8 5.8 convolution_convert_fusion.2
  450.8 5.8 convolution_convert_fusion.3
  460.4 8.0 collective-permute-start.42
  482.8 6.2 collective-permute-start.75
  489.0 5.4 add_convert_fusion.2
  495.5 5.4 add_convert_fusion.3
  514.6 5.8 collective-permute-done.35
  520.4 28.0 %collective-permute-done.36 = bf16[256,2048]{1,0:T(8,128)(2,1)S(1)} collective-permute-done((bf16[256,2048]{1,0:T(8,128)(2,1)S(1)}, bf16[256,2048]{1,0:T(8,128)(2,1)S(1)}, u32[]{:S(2)}, u32[]{:S(2)}) %collective-permute-start.36) | collective-permute-done | bytes 1048608 | tf_op jit(solution)/shard_map/ppermute | solution.py:398
  554.0 8.3 shard_map.260
  567.3 5.7 convolution_convert_fusion.10
  585.7 13.7 %shard_map.261 = (bf16[1024,640]{1,0:T(8,128)(2,1)S(1)}, bf16[1024,640]{1,0:T(8,128)(2,1)S(1)}, f32[1024,640]{1,0:T(8,128)S(1)}, f32[1,640]{1,0:T(1,128)S(1)}) custom-call(f32[1024,640]{1,0:T(8,128)} %copy-done.15, f32[8,640]{1,0:T(8,128)S(1)} %multiply_add_fusion.1.right_ref, f32[1024,1280]{1,0:T(8,128)} %fusion.42.zi_ref.zr_ref, ...), custom_call_target="tpu_custom_call" | custom-call | flops 26214400 | bytes 24181248 | tf_op jit(solution)/shard_map/pallas_call | solution.py:254
  606.5 10.5 %shard_map.262 = (bf16[1024,640]{1,0:T(8,128)(2,1)S(1)}, f32[8,640]{1,0:T(8,128)S(1)}) custom-call(f32[1024,640]{1,0:T(8,128)S(1)} %add_add_fusion.dconv_ref, f32[24,640]{1,0:T(8,128)S(1)} %convert_element_type.567.next_ref, f32[1024,640]{1,0:T(8,128)} %copy-done.2, f32[24,640]{1,0:T(8,128)S(1)} %copy-done.19, f32[1048,128]{1,0:T(8,128)S(1)} %broadcast_in_dim.23.mask_ref, ...), custom_call_target="tpu_custom_call" | custom-call | flops 26214400 | bytes 7254016 | tf_op jit(solution)/shard_map/pallas_call | solution.py:254
  635.0 5.7 concatenate.106
  684.8 6.7 collective-permute-done.62
  691.4 11.4 %collective-permute-start.81 = (bf16[80,2048]{1,0:T(8,128)(2,1)}, bf16[80,2048]{1,0:T(8,128)(2,1)}, u32[]{:S(2)}, u32[]{:S(2)}) collective-permute-start(bf16[80,2048]{1,0:T(8,128)(2,1)} %fusion.33), channel_id=1, source_target_pairs={{0,8},{1,9},{2,10},{3,11},{4,12},{5,13},{6,14},{7,15},{8,16},{9,17... | collective-permute-start | bytes 983048 | tf_op jit(solution)/shard_map/ppermute | solution.py:398
  732.9 7.7 collective-permute-done.40
  744.9 7.1 fusion.18
  752.0 10.9 %collective-permute-done.78 = bf16[256,3072]{1,0:T(8,128)(2,1)S(1)} collective-permute-done((bf16[256,3072]{1,0:T(8,128)(2,1)S(1)}, bf16[256,3072]{1,0:T(8,128)(2,1)S(1)}, u32[]{:S(2)}, u32[]{:S(2)}) %collective-permute-start.78) | collective-permute-done | bytes 1572896 | tf_op jit(solution)/shard_map/ppermute | solution.py:398
  767.8 12.0 %collective-permute-done.77 = bf16[192,2048]{1,0:T(8,128)(2,1)S(1)} collective-permute-done((bf16[192,2048]{1,0:T(8,128)(2,1)S(1)}, bf16[192,2048]{1,0:T(8,128)(2,1)S(1)}, u32[]{:S(2)}, u32[]{:S(2)}) %collective-permute-start.77) | collective-permute-done | bytes 786464 | tf_op jit(solution)/shard_map/ppermute | solution.py:398
  798.4 29.1 %collective-permute-done.79 = bf16[256,3072]{1,0:T(8,128)(2,1)S(1)} collective-permute-done((bf16[256,3072]{1,0:T(8,128)(2,1)S(1)}, bf16[256,3072]{1,0:T(8,128)(2,1)S(1)}, u32[]{:S(2)}, u32[]{:S(2)}) %collective-permute-start.79) | collective-permute-done | bytes 1572896 | tf_op jit(solution)/shard_map/ppermute | solution.py:398
  833.6 31.9 %collective-permute-done.53 = bf16[256,1280]{1,0:T(8,128)(2,1)S(1)} collective-permute-done((bf16[256,1280]{1,0:T(8,128)(2,1)S(1)}, bf16[256,1280]{1,0:T(8,128)(2,1)S(1)}, u32[]{:S(2)}, u32[]{:S(2)}) %collective-permute-start.53) | collective-permute-done | bytes 655392 | tf_op jit(solution)/shard_map/ppermute | solution.py:398
  870.8 28.7 %collective-permute-start.84 = (bf16[80,2048]{1,0:T(8,128)(2,1)}, bf16[80,2048]{1,0:T(8,128)(2,1)}, u32[]{:S(2)}, u32[]{:S(2)}) collective-permute-start(bf16[80,2048]{1,0:T(8,128)(2,1)} %add_convert_fusion.10), channel_id=1, source_target_pairs={{0,0},{4,4},{8,1},{12,5},{16,2},{20,6},{24,3},{28,7},{1,8},{5,12},... | collective-permute-start | bytes 983048 | tf_op jit(solution)/shard_map/ppermute | solution.py:398
  899.5 13.7 %collective-permute-done.54 = bf16[256,1280]{1,0:T(8,128)(2,1)S(1)} collective-permute-done((bf16[256,1280]{1,0:T(8,128)(2,1)S(1)}, bf16[256,1280]{1,0:T(8,128)(2,1)S(1)}, u32[]{:S(2)}, u32[]{:S(2)}) %collective-permute-start.54) | collective-permute-done | bytes 655392 | tf_op jit(solution)/shard_map/ppermute | solution.py:398
  918.2 47.5 %all-to-all-start = ((bf16[256,2,768]{2,1,0:T(2,128)(2,1)}), bf16[256,2,768]{2,1,0:T(2,128)(2,1)S(1)}, u32[]{:S(2)}, u32[]{:S(2)}) async-start(bf16[256,2,768]{2,1,0:T(2,128)(2,1)} %fusion.47), calls=%async_computation | async-start | bytes 1572864 | tf_op jit(solution)/shard_map/all_to_all | solution.py:477
  1010.1 5.1 reshape.303
  (566 shorter events, 410.9 us)
Async XLA Ops:
  3.1 31.7 %collective-permute-start = (bf16[128,1280]{1,0:T(8,128)(2,1)}, bf16[128,1280]{1,0:T(8,128)(2,1)}, u32[]{:S(2)}, u32[]{:S(2)}) collective-permute-start(bf16[128,1280]{1,0:T(8,128)(2,1)} %pad_maximum_fusion.11), channel_id=1, source_target_pairs={{0,1},{1,0},{2,3},{3,2},{4,5},{5,4},{6,7},{7,6},{8,9},{9,8},{10,11... | collective-permute-start | bytes 983048 | tf_op jit(solution)/shard_map/ppermute | solution.py:398
  4.4 32.2 %collective-permute-start.1 = (bf16[128,1280]{1,0:T(8,128)(2,1)}, bf16[128,1280]{1,0:T(8,128)(2,1)}, u32[]{:S(2)}, u32[]{:S(2)}) collective-permute-start(bf16[128,1280]{1,0:T(8,128)(2,1)} %pad_maximum_fusion.12), channel_id=1, source_target_pairs={{0,2},{1,3},{2,0},{3,1},{4,6},{5,7},{6,4},{7,5},{8,10},{9,11},{10,... | collective-permute-start | bytes 983048 | tf_op jit(solution)/shard_map/ppermute | solution.py:398
  6.6 31.6 %collective-permute-start.2 = (bf16[128,1280]{1,0:T(8,128)(2,1)}, bf16[128,1280]{1,0:T(8,128)(2,1)}, u32[]{:S(2)}, u32[]{:S(2)}) collective-permute-start(bf16[128,1280]{1,0:T(8,128)(2,1)} %pad_maximum_fusion.13), channel_id=1, source_target_pairs={{0,3},{1,2},{2,1},{3,0},{4,7},{5,6},{6,5},{7,4},{8,11},{9,10},{10,... | collective-permute-start | bytes 983048 | tf_op jit(solution)/shard_map/ppermute | solution.py:398
  41.0 49.8 %collective-permute-start.4 = (bf16[272,2048]{1,0:T(8,128)(2,1)}, bf16[272,2048]{1,0:T(8,128)(2,1)}, u32[]{:S(2)}, u32[]{:S(2)}) collective-permute-start(bf16[272,2048]{1,0:T(8,128)(2,1)} %pad_maximum_fusion.5.refs_0_), channel_id=1, source_target_pairs={{0,2},{1,3},{2,0},{3,1},{4,6},{5,7},{6,4},{7,5},{8,10},{9,11},{10,... | collective-permute-start | bytes 3342344 | tf_op jit(solution)/shard_map/ppermute | solution.py:398
  42.3 50.4 %collective-permute-start.5 = (bf16[272,2048]{1,0:T(8,128)(2,1)}, bf16[272,2048]{1,0:T(8,128)(2,1)}, u32[]{:S(2)}, u32[]{:S(2)}) collective-permute-start(bf16[272,2048]{1,0:T(8,128)(2,1)} %pad_maximum_fusion.5.refs_0_), channel_id=1, source_target_pairs={{0,3},{1,2},{2,1},{3,0},{4,7},{5,6},{6,5},{7,4},{8,11},{9,10},{10,... | collective-permute-start | bytes 3342344 | tf_op jit(solution)/shard_map/ppermute | solution.py:398
  57.0 68.9 %collective-permute-start.7 = (bf16[384,1280]{1,0:T(8,128)(2,1)}, bf16[384,1280]{1,0:T(8,128)(2,1)}, u32[]{:S(2)}, u32[]{:S(2)}) collective-permute-start(bf16[384,1280]{1,0:T(8,128)(2,1)} %constant_dynamic-update-slice_fusion.refs_0_), channel_id=1, source_target_pairs={{0,4},{1,5},{2,6},{3,7},{4,0},{5,1},{6,2},{7,3},{8,12},{9,13},{10,... | collective-permute-start | bytes 2949128 | tf_op jit(solution)/shard_map/ppermute | solution.py:398
  67.5 58.4 %collective-permute-start.8 = (bf16[384,1280]{1,0:T(8,128)(2,1)}, bf16[384,1280]{1,0:T(8,128)(2,1)}, u32[]{:S(2)}, u32[]{:S(2)}) collective-permute-start(bf16[384,1280]{1,0:T(8,128)(2,1)} %collective-permute-done.6.refs_1_), channel_id=1, source_target_pairs={{0,4},{1,5},{2,6},{3,7},{4,0},{5,1},{6,2},{7,3},{8,12},{9,13},{10,... | collective-permute-start | bytes 2949128 | tf_op jit(solution)/shard_map/ppermute | solution.py:398
  124.9 71.8 %collective-permute-start.23 = (bf16[192,3072]{1,0:T(8,128)(2,1)}, bf16[192,3072]{1,0:T(8,128)(2,1)}, u32[]{:S(2)}, u32[]{:S(2)}) collective-permute-start(bf16[192,3072]{1,0:T(8,128)(2,1)} %constant_dynamic-update-slice_fusion.3.refs_0_), channel_id=1, source_target_pairs={{0,8},{1,9},{2,10},{3,11},{4,12},{5,13},{6,14},{7,15},{8,16},{9,17... | collective-permute-start | bytes 3538952 | tf_op jit(solution)/shard_map/ppermute | solution.py:398
  193.6 44.2 %collective-permute-start.14 = (bf16[256,2048]{1,0:T(8,128)(2,1)}, bf16[256,2048]{1,0:T(8,128)(2,1)}, u32[]{:S(2)}, u32[]{:S(2)}) collective-permute-start(bf16[256,2048]{1,0:T(8,128)(2,1)} %convolution_convert_fusion.12), channel_id=1, source_target_pairs={{0,2},{1,3},{2,0},{3,1},{4,6},{5,7},{6,4},{7,5},{8,10},{9,11},{10,... | collective-permute-start | bytes 3145736 | tf_op jit(solution)/shard_map/ppermute | solution.py:398
  194.5 43.4 %collective-permute-start.15 = (bf16[256,2048]{1,0:T(8,128)(2,1)}, bf16[256,2048]{1,0:T(8,128)(2,1)}, u32[]{:S(2)}, u32[]{:S(2)}) collective-permute-start(bf16[256,2048]{1,0:T(8,128)(2,1)} %convolution_convert_fusion.11), channel_id=1, source_target_pairs={{0,1},{1,0},{2,3},{3,2},{4,5},{5,4},{6,7},{7,6},{8,9},{9,8},{10,11... | collective-permute-start | bytes 3145736 | tf_op jit(solution)/shard_map/ppermute | solution.py:398
  196.8 55.9 %collective-permute-start.25 = (bf16[192,3072]{1,0:T(8,128)(2,1)}, bf16[192,3072]{1,0:T(8,128)(2,1)}, u32[]{:S(2)}, u32[]{:S(2)}) collective-permute-start(bf16[192,3072]{1,0:T(8,128)(2,1)} %collective-permute-done.23.refs_2_), channel_id=1, source_target_pairs={{0,8},{1,9},{2,10},{3,11},{4,12},{5,13},{6,14},{7,15},{8,16},{9,17... | collective-permute-start | bytes 3538952 | tf_op jit(solution)/shard_map/ppermute | solution.py:398
  244.8 47.6 %collective-permute-start.17 = (bf16[256,2048]{1,0:T(8,128)(2,1)}, bf16[256,2048]{1,0:T(8,128)(2,1)}, u32[]{:S(2)}, u32[]{:S(2)}) collective-permute-start(bf16[256,2048]{1,0:T(8,128)(2,1)} %multiply_convert_fusion.2), channel_id=1, source_target_pairs={{0,2},{1,3},{2,0},{3,1},{4,6},{5,7},{6,4},{7,5},{8,10},{9,11},{10,... | collective-permute-start | bytes 3145736 | tf_op jit(solution)/shard_map/ppermute | solution.py:398
  245.9 46.4 %collective-permute-start.18 = (bf16[256,2048]{1,0:T(8,128)(2,1)}, bf16[256,2048]{1,0:T(8,128)(2,1)}, u32[]{:S(2)}, u32[]{:S(2)}) collective-permute-start(bf16[256,2048]{1,0:T(8,128)(2,1)} %multiply_convert_fusion.2), channel_id=1, source_target_pairs={{0,3},{1,2},{2,1},{3,0},{4,7},{5,6},{6,5},{7,4},{8,11},{9,10},{10,... | collective-permute-start | bytes 3145736 | tf_op jit(solution)/shard_map/ppermute | solution.py:398
  252.7 67.4 %collective-permute-start.27 = (bf16[192,3072]{1,0:T(8,128)(2,1)}, bf16[192,3072]{1,0:T(8,128)(2,1)}, u32[]{:S(2)}, u32[]{:S(2)}) collective-permute-start(bf16[192,3072]{1,0:T(8,128)(2,1)} %collective-permute-done.25.refs_4_), channel_id=1, source_target_pairs={{0,8},{1,9},{2,10},{3,11},{4,12},{5,13},{6,14},{7,15},{8,16},{9,17... | collective-permute-start | bytes 3538952 | tf_op jit(solution)/shard_map/ppermute | solution.py:398
  295.8 57.1 %collective-permute-start.22 = (bf16[192,3072]{1,0:T(8,128)(2,1)}, bf16[192,3072]{1,0:T(8,128)(2,1)S(1)}, u32[]{:S(2)}, u32[]{:S(2)}) collective-permute-start(bf16[192,3072]{1,0:T(8,128)(2,1)} %constant_dynamic-update-slice_fusion.3.refs_0_), channel_id=1, source_target_pairs={{0,4},{1,5},{2,6},{3,7},{4,0},{5,1},{6,2},{7,3},{8,12},{9,13},{10,... | collective-permute-start | bytes 3538952 | tf_op jit(solution)/shard_map/ppermute | solution.py:398
  295.8 48.3 %collective-permute-start.30 = (bf16[256,2048]{1,0:T(8,128)(2,1)}, bf16[256,2048]{1,0:T(8,128)(2,1)S(1)}, u32[]{:S(2)}, u32[]{:S(2)}) collective-permute-start(bf16[256,2048]{1,0:T(8,128)(2,1)} %bitcast.46), channel_id=1, source_target_pairs={{0,2},{1,3},{2,0},{3,1},{4,6},{5,7},{6,4},{7,5},{8,10},{9,11},{10,... | collective-permute-start | bytes 3145736 | tf_op jit(solution)/shard_map/ppermute | solution.py:398
  300.0 44.1 %collective-permute-start.31 = (bf16[256,2048]{1,0:T(8,128)(2,1)}, bf16[256,2048]{1,0:T(8,128)(2,1)S(1)}, u32[]{:S(2)}, u32[]{:S(2)}) collective-permute-start(bf16[256,2048]{1,0:T(8,128)(2,1)} %bitcast.46), channel_id=1, source_target_pairs={{0,3},{1,2},{2,1},{3,0},{4,7},{5,6},{6,5},{7,4},{8,11},{9,10},{10,... | collective-permute-start | bytes 3145736 | tf_op jit(solution)/shard_map/ppermute | solution.py:398
  318.8 34.1 %collective-permute-start.24 = (bf16[192,3072]{1,0:T(8,128)(2,1)}, bf16[192,3072]{1,0:T(8,128)(2,1)S(1)}, u32[]{:S(2)}, u32[]{:S(2)}) collective-permute-start(bf16[192,3072]{1,0:T(8,128)(2,1)} %collective-permute-done.23.refs_2_), channel_id=1, source_target_pairs={{0,4},{1,5},{2,6},{3,7},{4,0},{5,1},{6,2},{7,3},{8,12},{9,13},{10,... | collective-permute-start | bytes 3538952 | tf_op jit(solution)/shard_map/ppermute | solution.py:398
  320.1 32.8 %collective-permute-start.26 = (bf16[192,3072]{1,0:T(8,128)(2,1)}, bf16[192,3072]{1,0:T(8,128)(2,1)S(1)}, u32[]{:S(2)}, u32[]{:S(2)}) collective-permute-start(bf16[192,3072]{1,0:T(8,128)(2,1)} %collective-permute-done.25.refs_4_), channel_id=1, source_target_pairs={{0,4},{1,5},{2,6},{3,7},{4,0},{5,1},{6,2},{7,3},{8,12},{9,13},{10,... | collective-permute-start | bytes 3538952 | tf_op jit(solution)/shard_map/ppermute | solution.py:398
  424.1 47.6 %collective-permute-start.32 = (bf16[256,2048]{1,0:T(8,128)(2,1)}, bf16[256,2048]{1,0:T(8,128)(2,1)S(1)}, u32[]{:S(2)}, u32[]{:S(2)}) collective-permute-start(bf16[256,2048]{1,0:T(8,128)(2,1)} %fusion.19), channel_id=1, source_target_pairs={{0,3},{1,2},{2,1},{3,0},{4,7},{5,6},{6,5},{7,4},{8,11},{9,10},{10,... | collective-permute-start | bytes 3145736 | tf_op jit(solution)/shard_map/ppermute | solution.py:398
  425.4 47.9 %collective-permute-start.33 = (bf16[256,2048]{1,0:T(8,128)(2,1)}, bf16[256,2048]{1,0:T(8,128)(2,1)S(1)}, u32[]{:S(2)}, u32[]{:S(2)}) collective-permute-start(bf16[256,2048]{1,0:T(8,128)(2,1)} %fusion.20), channel_id=1, source_target_pairs={{0,2},{1,3},{2,0},{3,1},{4,6},{5,7},{6,4},{7,5},{8,10},{9,11},{10,... | collective-permute-start | bytes 3145736 | tf_op jit(solution)/shard_map/ppermute | solution.py:398
  426.2 47.1 %collective-permute-start.34 = (bf16[256,2048]{1,0:T(8,128)(2,1)}, bf16[256,2048]{1,0:T(8,128)(2,1)S(1)}, u32[]{:S(2)}, u32[]{:S(2)}) collective-permute-start(bf16[256,2048]{1,0:T(8,128)(2,1)} %fusion.21), channel_id=1, source_target_pairs={{0,1},{1,0},{2,3},{3,2},{4,5},{5,4},{6,7},{7,6},{8,9},{9,8},{10,11... | collective-permute-start | bytes 3145736 | tf_op jit(solution)/shard_map/ppermute | solution.py:398
  428.7 28.0 %collective-permute-start.74 = (bf16[192,2048]{1,0:T(8,128)(2,1)S(1)}, bf16[192,2048]{1,0:T(8,128)(2,1)S(1)}, u32[]{:S(2)}, u32[]{:S(2)}) collective-permute-start(bf16[192,2048]{1,0:T(8,128)(2,1)S(1)} %convolution_convert_fusion.14), channel_id=1, source_target_pairs={{0,4},{1,5},{2,6},{3,7},{4,0},{5,1},{6,2},{7,3},{8,12},{9,13},{10,... | collective-permute-start | bytes 2359304 | tf_op jit(solution)/shard_map/ppermute | solution.py:398
  429.9 27.9 %collective-permute-start.73 = (bf16[192,2048]{1,0:T(8,128)(2,1)S(1)}, bf16[192,2048]{1,0:T(8,128)(2,1)S(1)}, u32[]{:S(2)}, u32[]{:S(2)}) collective-permute-start(bf16[192,2048]{1,0:T(8,128)(2,1)S(1)} %convolution_convert_fusion.15), channel_id=1, source_target_pairs={{0,4},{1,5},{2,6},{3,7},{4,0},{5,1},{6,2},{7,3},{8,12},{9,13},{10,... | collective-permute-start | bytes 2359304 | tf_op jit(solution)/shard_map/ppermute | solution.py:398
  460.4 125.2 %collective-permute-start.42 = (f32[8,640]{1,0:T(8,128)S(1)}, f32[8,640]{1,0:T(8,128)S(1)}, u32[]{:S(2)}, u32[]{:S(2)}) collective-permute-start(f32[8,640]{1,0:T(8,128)S(1)} %slice.338), channel_id=1, source_target_pairs={{4,0},{5,1},{6,2},{7,3},{8,4},{9,5},{10,6},{11,7},{12,8},{13,9},{1... | collective-permute-start | bytes 61448 | tf_op jit(solution)/shard_map/ppermute | solution.py:398
  475.2 30.7 %collective-permute-start.67 = (bf16[256,3072]{1,0:T(8,128)(2,1)}, bf16[256,3072]{1,0:T(8,128)(2,1)S(1)}, u32[]{:S(2)}, u32[]{:S(2)}) collective-permute-start(bf16[256,3072]{1,0:T(8,128)(2,1)} %convolution_convert_fusion.3), channel_id=1, source_target_pairs={{0,4},{1,5},{2,6},{3,7},{4,0},{5,1},{6,2},{7,3},{8,12},{9,13},{10,... | collective-permute-start | bytes 4718600 | tf_op jit(solution)/shard_map/ppermute | solution.py:398
  482.8 29.1 %collective-permute-start.75 = (bf16[192,2048]{1,0:T(8,128)(2,1)S(1)}, bf16[192,2048]{1,0:T(8,128)(2,1)S(1)}, u32[]{:S(2)}, u32[]{:S(2)}) collective-permute-start(bf16[192,2048]{1,0:T(8,128)(2,1)S(1)} %copy-done.61), channel_id=1, source_target_pairs={{0,8},{1,9},{2,10},{3,11},{4,12},{5,13},{6,14},{7,15},{8,16},{9,17... | collective-permute-start | bytes 2359304 | tf_op jit(solution)/shard_map/ppermute | solution.py:398
  500.9 47.4 %collective-permute-start.36 = (bf16[256,2048]{1,0:T(8,128)(2,1)S(1)}, bf16[256,2048]{1,0:T(8,128)(2,1)S(1)}, u32[]{:S(2)}, u32[]{:S(2)}) collective-permute-start(bf16[256,2048]{1,0:T(8,128)(2,1)S(1)} %get-tuple-element.224), channel_id=1, source_target_pairs={{0,2},{1,3},{2,0},{3,1},{4,6},{5,7},{6,4},{7,5},{8,10},{9,11},{10,... | collective-permute-start | bytes 3145736 | tf_op jit(solution)/shard_map/ppermute | solution.py:398
  505.9 42.4 %collective-permute-start.37 = (bf16[256,2048]{1,0:T(8,128)(2,1)S(1)}, bf16[256,2048]{1,0:T(8,128)(2,1)S(1)}, u32[]{:S(2)}, u32[]{:S(2)}) collective-permute-start(bf16[256,2048]{1,0:T(8,128)(2,1)S(1)} %get-tuple-element.224), channel_id=1, source_target_pairs={{0,3},{1,2},{2,1},{3,0},{4,7},{5,6},{6,5},{7,4},{8,11},{9,10},{10,... | collective-permute-start | bytes 3145736 | tf_op jit(solution)/shard_map/ppermute | solution.py:398
  513.1 151.9 %collective-permute-start.76 = (bf16[192,2048]{1,0:T(8,128)(2,1)}, bf16[192,2048]{1,0:T(8,128)(2,1)}, u32[]{:S(2)}, u32[]{:S(2)}) collective-permute-start(bf16[192,2048]{1,0:T(8,128)(2,1)} %add_convert_fusion.7), channel_id=1, source_target_pairs={{0,8},{1,9},{2,10},{3,11},{4,12},{5,13},{6,14},{7,15},{8,16},{9,17... | collective-permute-start | bytes 2359304 | tf_op jit(solution)/shard_map/ppermute | solution.py:398
  671.4 57.9 %collective-permute-start.38 = (bf16[256,2048]{1,0:T(8,128)(2,1)}, bf16[256,2048]{1,0:T(8,128)(2,1)}, u32[]{:S(2)}, u32[]{:S(2)}) collective-permute-start(bf16[256,2048]{1,0:T(8,128)(2,1)} %convolution_convert_fusion.10), channel_id=1, source_target_pairs={{0,3},{1,2},{2,1},{3,0},{4,7},{5,6},{6,5},{7,4},{8,11},{9,10},{10,... | collective-permute-start | bytes 3145736 | tf_op jit(solution)/shard_map/ppermute | solution.py:398
  672.7 60.1 %collective-permute-start.39 = (bf16[256,2048]{1,0:T(8,128)(2,1)}, bf16[256,2048]{1,0:T(8,128)(2,1)}, u32[]{:S(2)}, u32[]{:S(2)}) collective-permute-start(bf16[256,2048]{1,0:T(8,128)(2,1)} %convolution_convert_fusion.9), channel_id=1, source_target_pairs={{0,2},{1,3},{2,0},{3,1},{4,6},{5,7},{6,4},{7,5},{8,10},{9,11},{10,... | collective-permute-start | bytes 3145736 | tf_op jit(solution)/shard_map/ppermute | solution.py:398
  675.8 34.9 %collective-permute-start.51 = (bf16[256,1280]{1,0:T(8,128)(2,1)}, bf16[256,1280]{1,0:T(8,128)(2,1)}, u32[]{:S(2)}, u32[]{:S(2)}) collective-permute-start(bf16[256,1280]{1,0:T(8,128)(2,1)} %convolution_convert_fusion.4), channel_id=1, source_target_pairs={{0,4},{1,5},{2,6},{3,7},{4,0},{5,1},{6,2},{7,3},{8,12},{9,13},{10,... | collective-permute-start | bytes 1966088 | tf_op jit(solution)/shard_map/ppermute | solution.py:398
  677.5 37.0 %collective-permute-start.50 = (bf16[256,1280]{1,0:T(8,128)(2,1)}, bf16[256,1280]{1,0:T(8,128)(2,1)}, u32[]{:S(2)}, u32[]{:S(2)}) collective-permute-start(bf16[256,1280]{1,0:T(8,128)(2,1)} %convolution_convert_fusion.5), channel_id=1, source_target_pairs={{0,4},{1,5},{2,6},{3,7},{4,0},{5,1},{6,2},{7,3},{8,12},{9,13},{10,... | collective-permute-start | bytes 1966088 | tf_op jit(solution)/shard_map/ppermute | solution.py:398
  723.2 39.7 %collective-permute-start.78 = (bf16[256,3072]{1,0:T(8,128)(2,1)S(1)}, bf16[256,3072]{1,0:T(8,128)(2,1)S(1)}, u32[]{:S(2)}, u32[]{:S(2)}) collective-permute-start(bf16[256,3072]{1,0:T(8,128)(2,1)S(1)} %copy-done.84), channel_id=1, source_target_pairs={{0,8},{1,9},{2,10},{3,11},{4,12},{5,13},{6,14},{7,15},{8,16},{9,17... | collective-permute-start | bytes 4718600 | tf_op jit(solution)/shard_map/ppermute | solution.py:398
  729.2 56.0 %collective-permute-start.45 = (bf16[256,2048]{1,0:T(8,128)(2,1)S(1)}, bf16[256,2048]{1,0:T(8,128)(2,1)S(1)}, u32[]{:S(2)}, u32[]{:S(2)}) collective-permute-start(bf16[256,2048]{1,0:T(8,128)(2,1)S(1)} %copy-done.58), channel_id=1, source_target_pairs={{0,3},{1,2},{2,1},{3,0},{4,7},{5,6},{6,5},{7,4},{8,11},{9,10},{10,... | collective-permute-start | bytes 3145736 | tf_op jit(solution)/shard_map/ppermute | solution.py:398
  729.3 55.9 %collective-permute-start.46 = (bf16[256,2048]{1,0:T(8,128)(2,1)S(1)}, bf16[256,2048]{1,0:T(8,128)(2,1)S(1)}, u32[]{:S(2)}, u32[]{:S(2)}) collective-permute-start(bf16[256,2048]{1,0:T(8,128)(2,1)S(1)} %copy-done.57), channel_id=1, source_target_pairs={{0,2},{1,3},{2,0},{3,1},{4,6},{5,7},{6,4},{7,5},{8,10},{9,11},{10,... | collective-permute-start | bytes 3145736 | tf_op jit(solution)/shard_map/ppermute | solution.py:398
  732.9 54.5 %collective-permute-start.47 = (bf16[256,2048]{1,0:T(8,128)(2,1)S(1)}, bf16[256,2048]{1,0:T(8,128)(2,1)S(1)}, u32[]{:S(2)}, u32[]{:S(2)}) collective-permute-start(bf16[256,2048]{1,0:T(8,128)(2,1)S(1)} %copy-done.56), channel_id=1, source_target_pairs={{0,1},{1,0},{2,3},{3,2},{4,5},{5,4},{6,7},{7,6},{8,9},{9,8},{10,11... | collective-permute-start | bytes 3145736 | tf_op jit(solution)/shard_map/ppermute | solution.py:398
  740.6 39.2 %collective-permute-start.77 = (bf16[192,2048]{1,0:T(8,128)(2,1)S(1)}, bf16[192,2048]{1,0:T(8,128)(2,1)S(1)}, u32[]{:S(2)}, u32[]{:S(2)}) collective-permute-start(bf16[192,2048]{1,0:T(8,128)(2,1)S(1)} %copy-done.62), channel_id=1, source_target_pairs={{0,8},{1,9},{2,10},{3,11},{4,12},{5,13},{6,14},{7,15},{8,16},{9,17... | collective-permute-start | bytes 2359304 | tf_op jit(solution)/shard_map/ppermute | solution.py:398
  762.9 30.9 %collective-permute-start.52 = (bf16[256,1280]{1,0:T(8,128)(2,1)S(1)}, bf16[256,1280]{1,0:T(8,128)(2,1)S(1)}, u32[]{:S(2)}, u32[]{:S(2)}) collective-permute-start(bf16[256,1280]{1,0:T(8,128)(2,1)S(1)} %fusion.25), channel_id=1, source_target_pairs={{0,8},{1,9},{2,10},{3,11},{4,12},{5,13},{6,14},{7,15},{8,16},{9,17... | collective-permute-start | bytes 1966088 | tf_op jit(solution)/shard_map/ppermute | solution.py:398
  779.7 47.8 %collective-permute-start.79 = (bf16[256,3072]{1,0:T(8,128)(2,1)S(1)}, bf16[256,3072]{1,0:T(8,128)(2,1)S(1)}, u32[]{:S(2)}, u32[]{:S(2)}) collective-permute-start(bf16[256,3072]{1,0:T(8,128)(2,1)S(1)} %add_convert_fusion.1), channel_id=1, source_target_pairs={{0,8},{1,9},{2,10},{3,11},{4,12},{5,13},{6,14},{7,15},{8,16},{9,17... | collective-permute-start | bytes 4718600 | tf_op jit(solution)/shard_map/ppermute | solution.py:398
  785.2 84.8 %collective-permute-start.83 = (bf16[80,2048]{1,0:T(8,128)(2,1)S(1)}, bf16[80,2048]{1,0:T(8,128)(2,1)S(1)}, u32[]{:S(2)}, u32[]{:S(2)}) collective-permute-start(bf16[80,2048]{1,0:T(8,128)(2,1)S(1)} %add_convert_fusion.11), channel_id=1, source_target_pairs={{0,8},{1,9},{2,10},{3,11},{4,12},{5,13},{6,14},{7,15},{8,16},{9,17... | collective-permute-start | bytes 983048 | tf_op jit(solution)/shard_map/ppermute | solution.py:398
  785.2 206.5 %collective-permute-start.85 = (bf16[192,2048]{1,0:T(8,128)(2,1)}, bf16[192,2048]{1,0:T(8,128)(2,1)}, u32[]{:S(2)}, u32[]{:S(2)}) collective-permute-start(bf16[192,2048]{1,0:T(8,128)(2,1)} %fusion.176), channel_id=1, source_target_pairs={{0,0},{4,4},{8,1},{12,5},{16,2},{20,6},{24,3},{28,7},{1,8},{5,12},... | collective-permute-start | bytes 2359304 | tf_op jit(solution)/shard_map/ppermute | solution.py:398
  794.0 71.5 %collective-permute-start.53 = (bf16[256,1280]{1,0:T(8,128)(2,1)S(1)}, bf16[256,1280]{1,0:T(8,128)(2,1)S(1)}, u32[]{:S(2)}, u32[]{:S(2)}) collective-permute-start(bf16[256,1280]{1,0:T(8,128)(2,1)S(1)} %add_convert_fusion.9), channel_id=1, source_target_pairs={{0,8},{1,9},{2,10},{3,11},{4,12},{5,13},{6,14},{7,15},{8,16},{9,17... | collective-permute-start | bytes 1966088 | tf_op jit(solution)/shard_map/ppermute | solution.py:398
  829.3 136.4 %collective-permute-start.80 = (bf16[256,3072]{1,0:T(8,128)(2,1)}, bf16[256,3072]{1,0:T(8,128)(2,1)}, u32[]{:S(2)}, u32[]{:S(2)}) collective-permute-start(bf16[256,3072]{1,0:T(8,128)(2,1)} %add_convert_fusion), channel_id=1, source_target_pairs={{0,8},{1,9},{2,10},{3,11},{4,12},{5,13},{6,14},{7,15},{8,16},{9,17... | collective-permute-start | bytes 4718600 | tf_op jit(solution)/shard_map/ppermute | solution.py:398
  865.6 47.6 %collective-permute-start.54 = (bf16[256,1280]{1,0:T(8,128)(2,1)S(1)}, bf16[256,1280]{1,0:T(8,128)(2,1)S(1)}, u32[]{:S(2)}, u32[]{:S(2)}) collective-permute-start(bf16[256,1280]{1,0:T(8,128)(2,1)S(1)} %add_convert_fusion.8), channel_id=1, source_target_pairs={{0,8},{1,9},{2,10},{3,11},{4,12},{5,13},{6,14},{7,15},{8,16},{9,17... | collective-permute-start | bytes 1966088 | tf_op jit(solution)/shard_map/ppermute | solution.py:398
  870.8 119.0 %collective-permute-start.84 = (bf16[80,2048]{1,0:T(8,128)(2,1)}, bf16[80,2048]{1,0:T(8,128)(2,1)}, u32[]{:S(2)}, u32[]{:S(2)}) collective-permute-start(bf16[80,2048]{1,0:T(8,128)(2,1)} %add_convert_fusion.10), channel_id=1, source_target_pairs={{0,0},{4,4},{8,1},{12,5},{16,2},{20,6},{24,3},{28,7},{1,8},{5,12},... | collective-permute-start | bytes 983048 | tf_op jit(solution)/shard_map/ppermute | solution.py:398
  918.2 62.7 %all-to-all-start = ((bf16[256,2,768]{2,1,0:T(2,128)(2,1)}), bf16[256,2,768]{2,1,0:T(2,128)(2,1)S(1)}, u32[]{:S(2)}, u32[]{:S(2)}) async-start(bf16[256,2,768]{2,1,0:T(2,128)(2,1)} %fusion.47), calls=%async_computation | async-start | bytes 1572864 | tf_op jit(solution)/shard_map/all_to_all | solution.py:477
  (136 other events, 2302.3 us)

commit v2 on v1

--- a/solution.py
+++ b/solution.py
@@ -301,39 +301,51 @@
     )(places, *blocks)
 
 
-def norm_rows(pieces, gain, rows):
-    width = pieces[0].shape[1]
+def norm_rows(values, count, rows, first_gain, order):
+    width = values.shape[1]
     step = 16
-
-    def kernel(gain_ref, *refs):
-        out_ref = refs[-1]
-        for i, ref in enumerate(refs[:-1]):
-
-            @pl.when(pl.program_id(0) == i)
-            def _():
-                def body(k, _):
-                    at = pl.ds(pl.multiple_of(k * step, step), step)
-                    v = ref[at, :].astype(f32)
-                    scale = lax.rsqrt(jnp.mean(v * v, axis=-1, keepdims=True) + EPS)
-                    out_ref[at, :] = (v * scale * gain_ref[0:1, :]).astype(bf16)
-                    return 0
-
-                lax.fori_loop(0, rows // step, body, 0)
+    stride = values.shape[0] // count
+    shard = width // count
+
+    def kernel(order_ref, ref, out_ref, one_ref, two_ref):
+        i = pl.program_id(0)
+
+        @pl.when(i == 0)
+        def _():
+            for k in range(count):
+                at = pl.ds(k * shard, shard)
+                note = ref[pl.ds(k * stride + rows, step), pl.ds(0, shard)].astype(f32)
+                one_ref[:, at] = jnp.broadcast_to(note[first_gain : first_gain + 1], (8, shard))
+                two_ref[:, at] = jnp.broadcast_to(note[first_gain + 1 : first_gain + 2], (8, shard))
+
+        def body(k, _):
+            v = ref[pl.ds(pl.multiple_of(i * stride + k * step, step), step), :].astype(f32)
+            scale = lax.rsqrt(jnp.mean(v * v, axis=-1, keepdims=True) + EPS)
+            at = pl.ds(pl.multiple_of(k * step, step), step)
+            out_ref[at, :] = (v * scale * one_ref[0:1, :]).astype(bf16)
+            return 0
+
+        lax.fori_loop(0, rows // step, body, 0, unroll=4)
 
     return pl.pallas_call(
         kernel,
-        grid=(len(pieces),),
-        in_specs=[pl.BlockSpec((8, width), lambda i: (0, 0))]
-        + [pl.BlockSpec(p.shape, lambda i: (0, 0)) for p in pieces],
-        out_specs=pl.BlockSpec((rows, width), lambda i: (i, 0)),
-        out_shape=jax.ShapeDtypeStruct((rows * len(pieces), width), bf16),
+        grid=(count,),
+        in_specs=[pl.BlockSpec(memory_space=pltpu.SMEM), pl.BlockSpec(values.shape, lambda i: (0, 0))],
+        out_specs=[
+            pl.BlockSpec((rows, width), lambda i: (i, 0)),
+            pl.BlockSpec((8, width), lambda i: (0, 0)),
+            pl.BlockSpec((8, width), lambda i: (0, 0)),
+        ],
+        out_shape=[
+            jax.ShapeDtypeStruct((rows * count, width), bf16),
+            jax.ShapeDtypeStruct((8, width), f32),
+            jax.ShapeDtypeStruct((8, width), f32),
+        ],
         compiler_params=pltpu.CompilerParams(vmem_limit_bytes=VMEM_LIMIT),
         cost_estimate=pl.CostEstimate(
-            flops=6 * rows * len(pieces) * width,
-            bytes_accessed=4 * rows * len(pieces) * width,
-            transcendentals=0,
+            flops=6 * rows * count * width, bytes_accessed=4 * rows * count * width, transcendentals=0
         ),
-    )(jnp.broadcast_to(gain[None, :], (8, width)), *pieces)
+    )(order, values)
 
 
 def after(value, *others):
@@ -388,27 +400,22 @@
     twin_perm = perm_of(lambda s: s ^ 1)
     pair_perm = perm_of(lambda s: s ^ 2)
     ring_perm = perm_of(lambda s: (s + 2) % seqs)
+    assert chips == wide
     from_owner = [(k // wide * wide + k % wide, k % seqs * wide + k // seqs) for k in range(seqs * wide)]
-    halves_to_owner = []
-    for w in range(wide):
-        for s in range(seqs):
-            halves_to_owner.append((s * wide + w, w * seqs + s % 2 * chips + s // 2))
+    to_owner = [(b, a) for a, b in from_owner]
 
     def send(value, perm):
         return lax.ppermute(value, AXES, perm)
 
-    def spread(piece):
-        return [piece] + [send(piece, along_wsh(r)) for r in range(1, wide)]
-
-    def collect(products):
-        got = [send(products[r].astype(bf16), along_wsh(r)) for r in range(wide - 1, 0, -1)]
-        total = products[0]
-        for value in got:
-            total = total + value.astype(f32)
-        return total
-
-    def token_rows(value, r):
-        return value[r * own : (r + 1) * own]
+    def exchange(rows):
+        return lax.all_to_all(rows, "wsh", split_axis=0, concat_axis=0, tiled=True)
+
+    def gather(rows):
+        return exchange(jnp.tile(rows, (wide, 1)))
+
+    def added(rows):
+        n = rows.shape[0] // wide
+        return sum(rows[w * n : (w + 1) * n].astype(f32) for w in range(wide))
 
     def own_columns(weights, r, start, rows):
         parts = []
@@ -420,7 +427,7 @@
 
     def fetch(weights, rows, at):
         got = [send(own_columns(weights, r, at * rows, rows), along_wsh(r)) for r in range(wide - 1, 0, -1)]
-        return jnp.concatenate(got[::-1], axis=0)
+        return got[::-1]
 
     def place(weights, fetched, rows):
         places = [(wsh ^ r) * shard + at * rows for _, at in fetched for r in range(1, wide)]
@@ -429,55 +436,55 @@
         out = assemble(places, blocks, D, rows, wide - 1, len(weights))
         return [value[:, : w.shape[1] // wide] for value, w in zip(out, weights)]
 
-    def pair_sums(terms):
-        pairs = []
-        for k in list(range(1, chips)) + [0]:
-            target = lax.rem(chip - k + chips, chips)
-            other = send(terms(target, 1 - core).astype(bf16), twin_perm)
-            pairs.append((terms(target, core) + other.astype(f32)).astype(bf16))
-        return list(lax.optimization_barrier(tuple(pairs)))
-
-    def ring_step(held, pair):
-        return send(held.astype(bf16), ring_perm).astype(f32) + pair.astype(f32)
-
-    def ring_sum(pairs):
-        held = pairs[0]
-        for pair in pairs[1:]:
-            held = ring_step(held, pair)
-        return held
-
-    def strided_terms(left, right):
+    def strided(left, half):
         n = left.shape[1] // seqs
-
-        def terms(target, half):
-            return t_dot(lax.dynamic_slice(left, (0, (2 * target + half) * n), (left.shape[0], n)), right)
-
-        return terms
-
-    def halved_terms(left, right):
-        n = left.shape[1] // seqs
-
-        def terms(target, half):
-            return t_dot(lax.dynamic_slice(left, (0, (half * chips + target) * n), (left.shape[0], n)), right)
-
-        return terms
+        return jnp.concatenate(
+            [lax.dynamic_slice(left, (0, (2 * k + half) * n), (left.shape[0], n)) for k in range(chips)], axis=1
+        )
+
+    def halved(left, half):
+        n = left.shape[1] // 2
+        return lax.dynamic_slice(left, (0, half * n), (left.shape[0], n))
+
+    def pair_terms(left, right, select):
+        other = t_dot(select(left, 1 - core), right).astype(bf16)
+        mine = t_dot(select(after(left, other), core), right).astype(bf16)
+        return mine, send(other, twin_perm)
+
+    def ring_chunk(pair, k):
+        rows = pair[0].shape[0] // chips
+        at = lax.rem(chip - k + chips, chips) * rows
+        mine, other = [lax.dynamic_slice(p, (at, 0), (rows, p.shape[1])) for p in pair]
+        return mine.astype(f32) + other.astype(f32)
+
+    def pair_total(pair):
+        return (pair[0].astype(f32) + pair[1].astype(f32)).astype(bf16)
+
+    def swapped_chunk(swapped, k):
+        rows = swapped.shape[0] // chips
+        at = lax.rem(chip - k + chips, chips) * rows
+        return lax.dynamic_slice(swapped, (at, 0), (rows, swapped.shape[1])).astype(f32)
+
+    def ring_step(held, chunk):
+        return send(held.astype(bf16), ring_perm).astype(f32) + chunk
 
     def columns_to_rows(value, weights, gain):
-        rows = value.shape[0]
-        weight_rows = [lax.dynamic_slice(w, (seq * rows, 0), (rows, w.shape[1])) for w in weights]
-        weight_rows = jnp.concatenate(weight_rows, axis=1).astype(f32)
+        rows, n = value.shape[0], value.shape[1] // 2
+        weight_rows = [lax.dynamic_slice(w, (seq * rows, 0), (rows, w.shape[1])).astype(f32) for w in weights]
         own_gain = lax.dynamic_slice(gain, (seq * rows,), (rows,))
-        term = jnp.sum(value * weight_rows, axis=1) / own_gain
-        low = value.astype(bf16).reshape(rows, 2, -1)
+        term = jnp.sum(value[:, :n] * weight_rows[0], axis=1) + jnp.sum(value[:, n:] * weight_rows[1], axis=1)
+        term = term / own_gain
         term_low = term.astype(bf16)
         rest = (term - term_low.astype(f32)).astype(bf16)
-        extra = jnp.pad(jnp.stack([term_low, rest], axis=1)[:, :, None], ((0, 0), (0, 0), (0, LANES - 1)))
-        n = low.shape[2]
-        low = jnp.concatenate([low, extra], axis=2)
-        got = lax.all_to_all(low, "wsh", split_axis=0, concat_axis=2, tiled=True).astype(f32)
-        got = got.reshape(rows // wide, 2, wide, n + LANES)
-        grads = got[:, :, :, :n].reshape(rows // wide, 2, wide * n)
-        return grads[:, 0], grads[:, 1], jnp.sum(got[:, :, :, n], axis=(1, 2))
+        extra = jnp.pad(jnp.stack([term_low, rest], axis=1), ((0, 0), (0, LANES - 2)))
+        low = jnp.concatenate([value.astype(bf16), extra], axis=1)
+
+        got = exchange(low).reshape(wide, rows // wide, low.shape[1])
+        grads = [
+            jnp.concatenate([got[w, :, k * n : (k + 1) * n].astype(f32) for w in range(wide)], axis=1) for k in range(2)
+        ]
+        total = jnp.sum(got[:, :, 2 * n : 2 * n + 2].astype(f32), axis=(0, 2))
+        return grads[0], grads[1], total
 
     def dot(a, b):
         return jnp.dot(a, b, preferred_element_type=f32)
@@ -496,18 +503,38 @@
         scaled = dn * gain
         return s * scaled - v * (s * s * s) * jnp.mean(scaled * v, axis=-1, keepdims=True)
 
+    def neighbours(weights, held):
+        here, there = seq % 4, seq % 4 ^ 2
+        paired = send(held, pair_perm)
+
+        def parts():
+            return [
+                (held, here),
+                (paired, there),
+                (send(held, twin_perm), here ^ 1),
+                (send(paired, twin_perm), there ^ 1),
+            ]
+
+        return paired, lambda: place(weights, parts(), shard // 4)
+
     branch = [gate_branch_w, linear_branch_w]
-    branch_rows = shard // 4
-    held = fetch(branch, branch_rows, seq % 4)
-    paired = send(held, pair_perm)
-    here, there = seq % 4, seq % 4 ^ 2
-    branch_parts = [
-        (held, here),
-        (paired, there),
-        (send(held, twin_perm), here ^ 1),
-        (send(paired, twin_perm), there ^ 1),
-    ]
-    w_gate, w_linear = place(branch, branch_parts, branch_rows)
+    held = fetch(branch, shard // 4, seq % 4)
+
+    small = jnp.concatenate([input_gate_w, recur_gate_w, conv_weight, decay_param[:, None]], axis=1)
+    pad = -small.shape[1] % LANES
+    small = send(jnp.pad(small, ((0, 0), (0, pad))), from_owner)
+    held, small = lax.optimization_barrier((held, small))
+    held = jnp.concatenate(held, axis=0)
+    _, place_branch = neighbours(branch, held)
+    w_gate, w_linear = place_branch()
+    small_rows = small.shape[0]
+    small = small[None]
+    for b in range(seqs.bit_length() - 1):
+        small = jnp.concatenate([small, send(small, perm_of(lambda s: s ^ (1 << b)))], axis=0)
+    joined = jnp.zeros((C, small.shape[2]), bf16)
+    for k in range(seqs):
+        joined = lax.dynamic_update_slice(joined, small[k], ((seq ^ k) * small_rows, 0))
+    small = joined
 
     rows = jnp.pad(segments[:, 0], ((0, 0), (taps - 1, taps - 1)), constant_values=-1)
     whole_depth = jnp.zeros((micro, length + taps - 1), f32)
@@ -522,23 +549,12 @@
     note = note.at[micro, :shard].set(norm1_gain)
     note = note.at[micro + 1, :shard].set(norm2_gain)
     noted = jnp.concatenate([inputs[:, 0].reshape(own, D), note], axis=0)
-    x_pieces = spread(after(noted, held))
-    notes = [piece[own:] for piece in x_pieces]
-    depth = jnp.concatenate([n[:micro, : T + taps - 1] for n in notes], axis=0).astype(f32)
+    x_group = gather(after(noted, held))
+    depth = x_group.reshape(wide, own + 16, D)[:, own : own + micro, : T + taps - 1]
+    depth = depth.reshape(Q, T + taps - 1).astype(f32)
     mask = jnp.broadcast_to(depth.T[:, :, None], (T + taps - 1, Q, LANES)).reshape(-1, LANES)
     mask_own = mask[: T * Q]
 
-    def joined(k):
-        whole = jnp.zeros((D,), bf16)
-        for r in range(wide):
-            whole = lax.dynamic_update_slice(whole, notes[r][micro + k, :shard], ((wsh ^ r) * shard,))
-        return whole.astype(f32)
-
-    gain_one, gain_two = joined(0), joined(1)
-    small = jnp.concatenate([input_gate_w, recur_gate_w, conv_weight, decay_param[:, None]], axis=1)
-    pad = -small.shape[1] % LANES
-    small = send(jnp.pad(small, ((0, 0), (0, pad))), from_owner)
-    small = lax.all_gather(small, "seq", axis=0, tiled=True)
     in_gate = small[:, :block]
     rec_gate = small[:, block : 2 * block]
     conv_w = small[:, 2 * block : 2 * block + taps].astype(f32).T
@@ -547,29 +563,26 @@
     soft = jnp.stack([jax.nn.softplus(-decay), jax.nn.sigmoid(-decay)])
     soft = jnp.pad(soft, ((0, 6), (0, 0)))
     blocks = C // block
-    eye = jnp.eye(blocks, dtype=bf16)
 
     def dense(gate_w):
-        spread_w = gate_w.reshape(blocks, block, 1, block) * eye[:, None, :, None]
-        return jnp.pad(spread_w.reshape(C, C), ((0, 0), (0, wide_C - C)))
+        slabs = []
+        for b in range(blocks):
+            slab = gate_w[b * block : (b + 1) * block]
+            slabs.append(jnp.pad(slab, ((0, 0), (b * block, wide_C - (b + 1) * block))))
+        return jnp.concatenate(slabs, axis=0)
 
     gates_w = jnp.concatenate([dense(in_gate), dense(rec_gate)], axis=1)
 
-    xn = norm_rows(x_pieces, gain_one, own)
+    order = after(jnp.zeros((1,), jnp.int32), w_gate, gates_w)
+    xn, gain_one, gain_two = norm_rows(x_group, wide, own, micro, order)
+    gain_one, gain_two = gain_one[0], gain_two[0]
     last = xn.reshape(Q, T, D)[:, T - (taps - 1) :].transpose(1, 0, 2).reshape((taps - 1) * Q, D)
     halo = send(dot(last, w_linear).astype(bf16), along_seq(1)).astype(f32)
     us_pre = dot(xn, w_linear)
 
     mlp = [mlp_gate_w, mlp_up_w]
-    mlp_rows = shard // seqs
-    held = fetch([after(w, *x_pieces[1:]) for w in mlp], mlp_rows, seq)
-    mlp_parts = []
-    for k in range(chips):
-        if k:
-            held = send(held, ring_perm)
-        source = lax.rem(chip - k + chips, chips) * 2
-        mlp_parts.append((held, source + core))
-        mlp_parts.append((send(held, twin_perm), source + 1 - core))
+    mlp_held = fetch([after(w, xn) for w in mlp], shard // 4, seq % 4)
+    g_group = gather(after(cotangent[:, 0].reshape(own, D), x_group))
 
     (conv,) = tiled_call(
         partial(conv_kernel, T, Q, taps),
@@ -585,6 +598,8 @@
     )
     reach = pl.cdiv(length // 4, T)
     ends = [send(end, along_seq(k)) for k in range(1, reach + 1)]
+    following_ends = [send(end[Q:], along_seq(-k)) for k in range(1, reach)]
+    ends, following_ends = lax.optimization_barrier((ends, following_ends))
     ypre = dot(after(xn, end), w_gate)
     carry, through = ends[0][:Q], ends[0][Q:]
     for value in ends[1:]:
@@ -596,39 +611,46 @@
         [((T * Q, C), f32), ((T * Q, C), bf16), ((T * Q, C), bf16)],
         [T * Q],
     )
-    following_ends = [send(end[Q:], along_seq(-k)) for k in range(1, reach)]
-
     x_own = inputs[:, 0].reshape(own, D).astype(f32)
-    hidden = x_own + collect([dot(token_rows(prod, r), out_proj_w) for r in range(wide)])
+    product, mlp_held, g_group = lax.optimization_barrier((dot(prod, out_proj_w).astype(bf16), mlp_held, g_group))
+    mlp_held = jnp.concatenate(mlp_held, axis=0)
+    mlp_paired, place_mlp = neighbours(mlp, mlp_held)
+    got, _ = lax.optimization_barrier((exchange(product), mlp_paired))
+    hidden = x_own + added(got)
     hn_own = (hidden * scale_of(hidden) * gain_two).astype(bf16)
-    hn_pieces = spread(hn_own)
-    hn = jnp.concatenate(hn_pieces, axis=0)
-    w_gate2, w_up = place(mlp, mlp_parts, mlp_rows)
-    g_pieces = spread(after(cotangent[:, 0].reshape(own, D), *hn_pieces[1:]))
-    gpre = dot(hn, w_gate2)
-    uppre = dot(hn, w_up)
-    act_gate, act_slope = gelu_parts(gpre)
-    act = (act_gate * uppre).astype(bf16)
-
-    g_group = jnp.concatenate(g_pieces, axis=0)
+    w_gate2, w_up = place_mlp()
+    hn, w_gate2, w_up = lax.optimization_barrier((gather(hn_own), w_gate2, w_up))
+    gpre = dot(hn, w_gate2).astype(bf16)
+    uppre = dot(hn, w_up).astype(bf16)
+    gpre, uppre = lax.optimization_barrier((gpre, uppre))
+    act = (gelu_parts(gpre.astype(f32))[0] * uppre.astype(f32)).astype(bf16)
+
     g_own = cotangent[:, 0].reshape(own, D).astype(f32)
-    dact = dot_t(g_group, mlp_down_w)
-    dgp = (dact * uppre * act_slope).astype(bf16)
+    down_pair = pair_terms(act, g_group, halved)
+    dact = dot_t(after(g_group, down_pair[0]), mlp_down_w)
+    act_gate, act_slope = gelu_parts(gpre.astype(f32))
+    dgp = (dact * uppre.astype(f32) * act_slope).astype(bf16)
     dup = (dact * act_gate).astype(bf16)
-    products = [dot_t(token_rows(dgp, r), w_gate2) + dot_t(token_rows(dup, r), w_up) for r in range(wide)]
-    products = [products[0]] + [p.astype(bf16) for p in products[1:]]
-    dhn = collect(products)
-    down_pairs = pair_sums(halved_terms(after(act, *products[1:]), g_group))
-    mlp_pairs = pair_sums(strided_terms(after(hn, *products[1:]), jnp.concatenate([dgp, dup], axis=1)))
-    down_sum = ring_sum(down_pairs)
-    mlp_sum = ring_sum([after(mlp_pairs[0], down_sum)] + mlp_pairs[1:])
-    dh1 = g_own + norm_back(dhn, hidden, gain_two)
-
-    do_own = dh1.astype(bf16)
-    do_pieces = spread(do_own)
-    do = jnp.concatenate(do_pieces, axis=0)
-    act_late = after(act, *do_pieces[1:])
-    block_output = hidden + collect([dot(token_rows(act_late, r), mlp_down_w) for r in range(wide)])
+    total, dgp, dup = lax.optimization_barrier((pair_total(down_pair), dgp, dup))
+    down = exchange(total)
+    product = (dot_t(dgp, w_gate2) + dot_t(dup, w_up)).astype(bf16)
+
+    def down_step(k, held):
+        return ring_step(held, swapped_chunk(down, k)) if k <= chips else held
+
+    down_sum = swapped_chunk(down, 1).astype(bf16)
+    product, down_sum, hn, dgp, dup = lax.optimization_barrier((product, down_sum, hn, dgp, dup))
+    mlp_terms = t_dot(hn, jnp.concatenate([dgp, dup], axis=1)).astype(bf16)
+    got, down_sum, mlp_terms = lax.optimization_barrier((exchange(product), down_step(2, down_sum), mlp_terms))
+    mlp_sum = lax.psum_scatter(mlp_terms, "seq", scatter_dimension=0, tiled=True).astype(f32)
+    dh1 = g_own + norm_back(added(got), hidden, gain_two)
+
+    do_own, act_late = lax.optimization_barrier((dh1.astype(bf16), act))
+    product = dot(act_late, mlp_down_w).astype(bf16)
+    do, down_sum, product = lax.optimization_barrier((gather(do_own), down_step(3, down_sum), product))
+    got = exchange(product)
+    for k in range(4, chips + 1):
+        down_sum = down_step(k, down_sum)
     dprod = dot_t(do, out_proj_w)
     dy, e_local, first = tiled_call(
         partial(back_scan_kernel, T, Q),
@@ -637,7 +659,7 @@
         [T * Q],
     )
     firsts = [send(first, along_seq(-k)) for k in range(1, reach + 1)]
-    out_pairs = pair_sums(halved_terms(after(prod, first), do))
+    out_terms = t_dot(after(prod, first), do).astype(bf16)
     right, through = firsts[0], None
     for value, past in zip(firsts[1:], following_ends):
         through = past if through is None else through * past
@@ -660,6 +682,7 @@
     )
     dconv = dconv_direct + dot_t(dzi, gates_w[:, :C]) + dot_t(dzr, gates_w[:, wide_C : wide_C + C])
     following = send(dconv[: (taps - 1) * Q].astype(bf16), along_seq(-1)).astype(f32)
+    following, got, down_sum = lax.optimization_barrier((following, got, down_sum))
     dus, dconv_w = tiled_call(
         partial(back_conv_kernel, T, Q, taps),
         [(dconv, 0), (following, 0), (us_pre, 0), (halo, 0), (mask, None), (conv_w, 0)],
@@ -667,23 +690,19 @@
         [T * Q],
     )
 
-    products = [dot_t(token_rows(dy, r), w_gate) + dot_t(token_rows(dus, r), w_linear) for r in range(wide)]
-    products = [products[0]] + [p.astype(bf16) for p in products[1:]]
-    dxn = collect(products)
-    branch_pairs = pair_sums(strided_terms(after(xn, *products[1:]), jnp.concatenate([dy, dus], axis=1)))
-    out_sum = ring_sum([after(out_pairs[0], mlp_sum)] + out_pairs[1:])
-    branch_sum = ring_sum(branch_pairs)
+    block_output = hidden + added(got)
+    branch_pair = pair_terms(xn, jnp.concatenate([dy, dus], axis=1), strided)
+    branch_sum = ring_chunk(branch_pair, 1).astype(bf16)
 
     def diagonal(terms):
         return jnp.concatenate(
             [terms[b * block : (b + 1) * block, b * block : (b + 1) * block] for b in range(blocks)], axis=0
         )
 
-    late_low = after(conv_low, *products[1:])
     small_terms = jnp.concatenate(
         [
-            diagonal(t_dot(late_low, dzi)),
-            diagonal(t_dot(late_low, dzr)),
+            diagonal(t_dot(conv_low, dzi)),
+            diagonal(t_dot(conv_low, dzr)),
             dconv_w[:taps].T,
             ddecay.T,
             jnp.zeros((C, pad), f32),
@@ -691,18 +710,23 @@
         axis=1,
     )
 
-    def small_chunk(target, half):
-        n = C // seqs
-        return lax.dynamic_slice(small_terms, ((half * chips + target) * n, 0), (n, small_terms.shape[1]))
-
-    small_sum = ring_sum(pair_sums(small_chunk))
+    def branch_step(k, held):
+        return ring_step(held, ring_chunk(branch_pair, k)) if k <= chips else held
+
+    dy_late, dus_late, branch_sum, small_terms = lax.optimization_barrier((dy, dus, branch_sum, small_terms))
+    row_terms = jnp.concatenate([out_terms, small_terms.astype(bf16)], axis=1)
+    row_sum = lax.psum_scatter(row_terms, "seq", scatter_dimension=0, tiled=True)
+    product = (dot_t(dy_late, w_gate) + dot_t(dus_late, w_linear)).astype(bf16)
+    product, branch_sum = lax.optimization_barrier((product, branch_step(2, branch_sum)))
+    got = exchange(product)
+    for k in range(3, chips + 1):
+        branch_sum = branch_step(k, branch_sum)
+    got, branch_sum = lax.optimization_barrier((got, branch_sum))
+    dxn = added(got)
+    row_sum = send(after(row_sum, got), to_owner).astype(f32)
+    out_sum, small_sum = row_sum[:, :D], row_sum[:, D:]
     input_grad = dh1 + norm_back(dxn, x_own, gain_one)
-
-    def owned(value):
-        return send(value.astype(bf16), halves_to_owner).astype(f32)
-
-    small_grad = owned(small_sum)
-    gate2_grad, up_grad, gain_two_grad = columns_to_rows(mlp_sum, [w_gate2, w_up], gain_two)
+    gate2_grad, up_grad, gain_two_grad = columns_to_rows(after(mlp_sum, got), [w_gate2, w_up], gain_two)
     gate_grad, linear_grad, gain_one_grad = columns_to_rows(branch_sum, [w_gate, w_linear], gain_one)
     return (
         block_output.reshape(inputs.shape),
@@ -710,15 +734,15 @@
         gain_one_grad,
         gate_grad,
         linear_grad,
-        small_grad[:, 2 * block : 2 * block + taps],
-        small_grad[:, :block],
-        small_grad[:, block : 2 * block],
-        small_grad[:, 2 * block + taps],
-        owned(out_sum),
+        small_sum[:, 2 * block : 2 * block + taps],
+        small_sum[:, :block],
+        small_sum[:, block : 2 * block],
+        small_sum[:, 2 * block + taps],
+        out_sum,
         gain_two_grad,
         gate2_grad,
         up_grad,
-        owned(down_sum),
+        down_sum,
     )
 
 

time: 1030 us -> 811 us (0.79)
  the two profiles are of different devices: /device:TPU:26 before, /device:TPU:0 now
where the time goes in v2:
time: 811 us; the launch traced here: 804 us
  waiting for transfers between devices  288 us (36%)
  matrix products  163 us (20%)
  starting transfers between devices  100 us (12%)
  other arithmetic  96.8 us (12%)
  Pallas kernels  70.6 us (9%)
  local copies, waits for them, and re-layouts  68.8 us (8%)
  between operations  16.3 us (2%)
    ppermute x32, waiting for transfers between devices, send(): return lax.ppermute(value, AXES, perm)  194 us
    all_to_all x11, waiting for transfers between devices, exchange(): return lax.all_to_all(rows, 'wsh', split_axis=0, concat_axis=0, tiled=True)  94 us
    dot_general x8, matrix products, dot_t(): lax.dot_general(a, b, (((1,), (1,)), ((), ())), preferred_element_type=f32)  55 us
    dot_general x8, matrix products, dot(): return jnp.dot(a, b, preferred_element_type=f32)  54.5 us
    all_to_all x11, starting transfers between devices, exchange(): return lax.all_to_all(rows, 'wsh', split_axis=0, concat_axis=0, tiled=True)  54.4 us
    dot_general x8, matrix products, t_dot(): lax.dot_general(a, b, (((0,), (0,)), ((), ())), preferred_element_type=f32)  53.9 us
    pallas_call x6, Pallas kernels, tiled_call(): pl.pallas_call(kernel, grid=(pl.cdiv(channels, LANES),), in_specs=[spec(a...  51.1 us
    ppermute x32, starting transfers between devices, send(): return lax.ppermute(value, AXES, perm)  45.4 us
  transfers between devices with their start and end apart: 45, of which 19 were waited for; matrix products, arithmetic and copies ran while one was open for 31% of the time, Pallas kernels for 8%

profile of v2, /device:TPU:0, one launch (start us, length us, event | category | flops | bytes accessed | tf_op | source)
XLA Modules:
  0.0 804.4 jit_solution(16711193848062861185)
XLA Ops:
  19.8 10.0 %collective-permute-done.1 = bf16[128,1280]{1,0:T(8,128)(2,1)S(1)} collective-permute-done((bf16[128,1280]{1,0:T(8,128)(2,1)}, bf16[128,1280]{1,0:T(8,128)(2,1)S(1)}, u32[]{:S(2)}, u32[]{:S(2)}) %collective-permute-start.1) | collective-permute-done | bytes 327712 | tf_op jit(solution)/shard_map/ppermute | solution.py:408
  38.7 5.4 all-to-all-start
  61.9 19.3 %collective-permute-done.9 = bf16[4,80,384]{1,2,0:T(8,128)(2,1)} collective-permute-done((bf16[4,80,384]{1,2,0:T(8,128)(2,1)}, bf16[4,80,384]{1,2,0:T(8,128)(2,1)}, u32[]{:S(2)}, u32[]{:S(2)}) %collective-permute-start.9) | collective-permute-done | bytes 245792 | tf_op jit(solution)/shard_map/ppermute | solution.py:408
  86.1 10.1 %maximum_maximum_fusion = bf16[640,1280]{0,1:T(8,128)(2,1)} fusion(bf16[160,640]{0,1:T(8,128)(2,1)S(1)} %pad.73, bf16[160,640]{0,1:T(8,128)(2,1)S(1)} %pad.72, bf16[160,640]{0,1:T(8,128)(2,1)S(1)} %pad.71, bf16[160,640]{0,1:T(8,128)(2,1)S(1)} %pad.70, bf16[160,640]{0,1:T(8,128)(2,1)S(1)} %pad.69, bf16[160,640]{0,1:T(8,128)(2,1)S(1)} %pad.68, ...), kind=kLoop, calls=%fused_computation.73 | loop fusion | flops 13107200 | bytes 3276800 | tf_op jit(solution)/shard_map/concatenate | solution.py:574
  96.3 4.9 shard_map.254
  101.2 4.9 shard_map.255
  129.0 8.0 fusion.99.pre_ref
  148.5 7.9 shard_map.257
  156.4 5.2 collective-permute-start.11
  165.6 6.7 fusion.100.ypre_ref
  174.1 6.9 shard_map.258
  181.1 5.0 convolution_convert_fusion.4
  186.1 9.4 %collective-permute-done.14 = bf16[128,3072]{1,0:T(8,128)(2,1)} collective-permute-done((bf16[128,3072]{1,0:T(8,128)(2,1)S(1)}, bf16[128,3072]{1,0:T(8,128)(2,1)}, u32[]{:S(2)}, u32[]{:S(2)}) %collective-permute-start.14) | collective-permute-done | bytes 786464 | tf_op jit(solution)/shard_map/ppermute | solution.py:408
  195.5 5.1 all-to-all-start.2
  209.5 51.2 %collective-permute-done.17.refs_1_ = bf16[384,3072]{1,0:T(8,128)(2,1)} collective-permute-done((bf16[384,3072]{1,0:T(8,128)(2,1)S(1)}, bf16[384,3072]{1,0:T(8,128)(2,1)}, u32[]{:S(2)}, u32[]{:S(2)}) %collective-permute-start.17) | collective-permute-done | bytes 2359328 | tf_op jit(solution)/shard_map/ppermute | solution.py:408
  268.2 4.9 all-to-all-start.3
  281.4 9.6 %shard_map.259 = (bf16[2048,1536]{1,0:T(8,128)(2,1)}, bf16[2048,1536]{1,0:T(8,128)(2,1)}) custom-call(s32[13]{0:T(128)S(1)} %stack.84.places_ref, bf16[384,3072]{1,0:T(8,128)(2,1)S(1)} %copy-done.14, bf16[384,3072]{1,0:T(8,128)(2,1)} %collective-permute-done.17.refs_1_, bf16[384,3072]{1,0:T(8,128)(2,1)} %collective-permute-done.18.refs_2_, ...), custom_call_target="tpu_custom_call" | custom-call | bytes 25165824 | tf_op jit(solution)/shard_map/pallas_call | solution.py:291
  291.0 29.1 %all-to-all-done.3 = bf16[4,256,2048]{2,1,0:T(8,128)(2,1)} async-done(((bf16[4,256,2048]{2,1,0:T(8,128)(2,1)}), bf16[4,256,2048]{2,1,0:T(8,128)(2,1)}, u32[]{:S(2)}, u32[]{:S(2)}) %all-to-all-start.3) | async-done | bytes 4194336 | tf_op jit(solution)/shard_map/all_to_all | solution.py:411
  320.1 10.1 %convolution_convert_fusion.2 = bf16[1024,1536]{1,0:T(8,128)(2,1)S(1)} fusion(bf16[1024,2048]{1,0:T(8,128)(2,1)} %bitcast.36, bf16[2048,1536]{1,0:T(8,128)(2,1)} %get-tuple-element.158), kind=kOutput, calls=%fused_computation.30 | convolution fusion | flops 6444023808 | bytes 13631488 | tf_op jit(solution)/shard_map/dot_general | solution.py:490
  330.2 8.5 %convolution_convert_fusion.3 = bf16[1024,1536]{1,0:T(8,128)(2,1)S(1)} fusion(bf16[1024,2048]{1,0:T(8,128)(2,1)} %bitcast.36, bf16[2048,1536]{1,0:T(8,128)(2,1)S(1)} %copy-done.74), kind=kOutput, calls=%fused_computation.31 | convolution fusion | flops 6444023808 | bytes 13631488 | tf_op jit(solution)/shard_map/dot_general | solution.py:490
  341.4 8.3 %convolution_convert_fusion.8 = bf16[768,2048]{1,0:T(8,128)(2,1)} fusion(bf16[1024,2048]{1,0:T(8,128)(2,1)} %bitcast.32, bf16[1024,1536]{1,0:T(8,128)(2,1)S(1)} %fusion, s32[]{:T(128)S(6)} %select_n.196), kind=kOutput, calls=%fused_computation.36 | convolution fusion | flops 3222798336 | bytes 8912900 | tf_op jit(solution)/shard_map/dot_general | solution.py:496
  349.7 6.1 convolution_convert_fusion.7
  355.8 15.3 %multiply_convert_fusion = (bf16[1024,1536]{1,0:T(8,128)(2,1)}, bf16[1024,1536]{1,0:T(8,128)(2,1)}) fusion(bf16[1024,1536]{1,0:T(8,128)(2,1)S(1)} %convolution_convert_fusion.3, bf16[1024,1536]{1,0:T(8,128)(2,1)S(1)} %convolution_convert_fusion.2, bf16[1024,2048]{1,0:T(8,128)(2,1)} %bitcast.32, bf16[1536,2048]{1,0:T(8,128)(2,1)S(1)} %bitcast.203), kind=kOutput, calls=%fused_computation.26 | convolution fusion | flops 6481772544 | bytes 23068672 | tf_op jit(solution)/shard_map/dot_general | solution.py:493
  378.9 9.9 %fusion.101 = f32[1024,2048]{1,0:T(8,128)S(1)} fusion(bf16[1024,1536]{1,0:T(8,128)(2,1)} %get-tuple-element.171, bf16[2048,1536]{1,0:T(8,128)(2,1)} %get-tuple-element.158), kind=kOutput, calls=%fused_computation.256 | convolution fusion | flops 6442450944 | bytes 17825792 | tf_op jit(solution)/shard_map/dot_general | solution.py:493
  388.8 11.1 %add_convert_fusion.1 = bf16[1024,2048]{1,0:T(8,128)(2,1)} fusion(f32[1024,2048]{1,0:T(8,128)S(1)} %fusion.101, bf16[1024,1536]{1,0:T(8,128)(2,1)S(1)} %copy-done.87, bf16[2048,1536]{1,0:T(8,128)(2,1)} %get-tuple-element.157), kind=kOutput, calls=%fused_computation.10 | convolution fusion | flops 6446645248 | bytes 22020096 | tf_op jit(solution)/shard_map/dot_general | solution.py:493
  399.9 15.9 %all-to-all-done.4 = bf16[4,192,2048]{2,1,0:T(8,128)(2,1)} async-done(((bf16[4,192,2048]{2,1,0:T(8,128)(2,1)}), bf16[4,192,2048]{2,1,0:T(8,128)(2,1)}, u32[]{:S(2)}, u32[]{:S(2)}) %all-to-all-start.4) | async-done | bytes 3145760 | tf_op jit(solution)/shard_map/all_to_all | solution.py:411
  417.9 4.9 all-to-all-start.5
  424.4 19.9 %convolution_convert_fusion = bf16[2048,3072]{1,0:T(8,128)(2,1)} fusion(bf16[1024,2048]{1,0:T(8,128)(2,1)} %bitcast.36, bf16[1024,1536]{1,0:T(8,128)(2,1)} %get-tuple-element.171, bf16[1024,1536]{1,0:T(8,128)(2,1)} %get-tuple-element.170), kind=kOutput, calls=%fused_computation.8 | convolution fusion | flops 12903776256 | bytes 23068672 | tf_op jit(solution)/shard_map/dot_general | solution.py:496
  446.7 23.5 %all-to-all-done.5 = bf16[4,256,2048]{2,1,0:T(8,128)(2,1)} async-done(((bf16[4,256,2048]{2,1,0:T(8,128)(2,1)}), bf16[4,256,2048]{2,1,0:T(8,128)(2,1)}, u32[]{:S(2)}, u32[]{:S(2)}) %all-to-all-start.5) | async-done | bytes 4194336 | tf_op jit(solution)/shard_map/all_to_all | solution.py:411
  474.0 5.6 fusion.90
  482.1 4.9 all-to-all-start.6
  488.6 11.1 %convolution_convert_fusion.1 = bf16[1024,2048]{1,0:T(8,128)(2,1)} fusion(bf16[1024,1536]{1,0:T(8,128)(2,1)} %copy-done.46, bf16[1536,2048]{1,0:T(8,128)(2,1)} %param.35), kind=kOutput, calls=%fused_computation.29 | convolution fusion | flops 6444548096 | bytes 13631488 | tf_op jit(solution)/shard_map/dot_general | solution.py:490
  499.6 25.8 %collective-permute-done.22 = bf16[192,2048]{1,0:T(8,128)(2,1)S(1)} collective-permute-done((bf16[192,2048]{1,0:T(8,128)(2,1)}, bf16[192,2048]{1,0:T(8,128)(2,1)S(1)}, u32[]{:S(2)}, u32[]{:S(2)}) %collective-permute-start.22) | collective-permute-done | bytes 786464 | tf_op jit(solution)/shard_map/ppermute | solution.py:408
  527.7 5.3 all-to-all-done.6
  533.1 5.1 all-to-all-start.7
  538.2 7.4 fusion.102.dprod_ref
  545.6 8.3 %shard_map.260 = (bf16[1024,640]{1,0:T(8,128)(2,1)S(1)}, f32[1024,640]{1,0:T(8,128)S(1)}, f32[8,640]{1,0:T(8,128)S(1)}) custom-call(f32[1024,640]{1,0:T(8,128)} %fusion.102.dprod_ref, f32[1024,640]{1,0:T(8,128)} %fusion.100.ypre_ref, bf16[1024,640]{1,0:T(8,128)(2,1)S(1)} %copy-done.19, f32[1024,640]{1,0:T(8,128)} %copy-done.6), custom_call_target="tpu_custom_call" | custom-call | flops 26214400 | bytes 13127680 | tf_op jit(solution)/shard_map/pallas_call | solution.py:254
  565.0 13.7 %shard_map.261 = (bf16[1024,640]{1,0:T(8,128)(2,1)S(1)}, bf16[1024,640]{1,0:T(8,128)(2,1)S(1)}, f32[1024,640]{1,0:T(8,128)S(1)}, f32[1,640]{1,0:T(1,128)S(1)}) custom-call(f32[1024,640]{1,0:T(8,128)} %copy-done.17, f32[8,640]{1,0:T(8,128)S(1)} %multiply_add_fusion.right_ref, f32[1024,1280]{1,0:T(8,128)} %fusion.84.zi_ref.zr_ref, ...), custom_call_target="tpu_custom_call" | custom-call | flops 26214400 | bytes 24181248 | tf_op jit(solution)/shard_map/pallas_call | solution.py:254
  587.0 13.7 %collective-permute-done.26 = bf16[192,2048]{1,0:T(8,128)(2,1)S(1)} collective-permute-done((bf16[192,2048]{1,0:T(8,128)(2,1)}, bf16[192,2048]{1,0:T(8,128)(2,1)S(1)}, u32[]{:S(2)}, u32[]{:S(2)}) %collective-permute-start.26) | collective-permute-done | bytes 786464 | tf_op jit(solution)/shard_map/ppermute | solution.py:408
  605.2 10.9 %shard_map.262 = (bf16[1024,640]{1,0:T(8,128)(2,1)S(1)}, f32[8,640]{1,0:T(8,128)S(1)}) custom-call(f32[1024,640]{1,0:T(8,128)S(1)} %copy-done.4, f32[24,640]{1,0:T(8,128)S(1)} %convert_element_type.466.next_ref, f32[1024,640]{1,0:T(8,128)} %fusion.99.pre_ref, f32[24,640]{1,0:T(8,128)S(1)} %copy-done.27, f32[1048,128]{1,0:T(8,128)S(1)} %broadcast_in_dim.39.mask_ref, ...), custom_call_target="tpu_custom_call" | custom-call | flops 26214400 | bytes 7254016 | tf_op jit(solution)/shard_map/pallas_call | solution.py:254
  643.0 5.1 add_convert_fusion
  648.1 9.7 %collective-permute-done.28 = bf16[256,1280]{1,0:T(8,128)(2,1)S(1)} collective-permute-done((bf16[256,1280]{1,0:T(8,128)(2,1)S(1)}, bf16[256,1280]{1,0:T(8,128)(2,1)S(1)}, u32[]{:S(2)}, u32[]{:S(2)}) %collective-permute-start.28) | collective-permute-done | bytes 655392 | tf_op jit(solution)/shard_map/ppermute | solution.py:408
  665.0 7.0 convolution_convert_fusion.9
  678.4 16.4 %collective-permute-done.29 = bf16[256,1280]{1,0:T(8,128)(2,1)} collective-permute-done((bf16[256,1280]{1,0:T(8,128)(2,1)}, bf16[256,1280]{1,0:T(8,128)(2,1)}, u32[]{:S(2)}, u32[]{:S(2)}) %collective-permute-start.29) | collective-permute-done | bytes 655392 | tf_op jit(solution)/shard_map/ppermute | solution.py:408
  697.5 5.0 add_add_fusion.1
  702.4 27.0 %collective-permute-done.30 = bf16[256,1280]{1,0:T(8,128)(2,1)} collective-permute-done((bf16[256,1280]{1,0:T(8,128)(2,1)}, bf16[256,1280]{1,0:T(8,128)(2,1)}, u32[]{:S(2)}, u32[]{:S(2)}) %collective-permute-start.30) | collective-permute-done | bytes 655392 | tf_op jit(solution)/shard_map/ppermute | solution.py:408
  736.4 5.4 all-to-all-start.9
  771.6 20.2 %all-to-all-done.10 = bf16[4,64,3200]{2,1,0:T(8,128)(2,1)} async-done(((bf16[4,64,3200]{2,1,0:T(8,128)(2,1)}), bf16[4,64,3200]{2,1,0:T(8,128)(2,1)}, u32[]{:S(2)}, u32[]{:S(2)}) %all-to-all-start.10) | async-done | bytes 1638432 | tf_op jit(solution)/shard_map/all_to_all | solution.py:411
  (414 shorter events, 243.2 us)
Async XLA Ops:
  7.2 173.9 %copy-start = (bf16[640,2048]{1,0:T(8,128)(2,1)S(1)}, bf16[640,2048]{1,0:T(8,128)(2,1)}, u32[]{:S(2)}) copy-start(bf16[640,2048]{1,0:T(8,128)(2,1)} %param.31) | copy-start | bytes 7864324
  10.5 19.4 %collective-permute-start.1 = (bf16[128,1280]{1,0:T(8,128)(2,1)}, bf16[128,1280]{1,0:T(8,128)(2,1)S(1)}, u32[]{:S(2)}, u32[]{:S(2)}) collective-permute-start(bf16[128,1280]{1,0:T(8,128)(2,1)} %pad_maximum_fusion.11), channel_id=1, source_target_pairs={{0,2},{1,3},{2,0},{3,1},{4,6},{5,7},{6,4},{7,5},{8,10},{9,11},{10,... | collective-permute-start | bytes 983048 | tf_op jit(solution)/shard_map/ppermute | solution.py:408
  14.2 15.7 %collective-permute-start.2 = (bf16[128,1280]{1,0:T(8,128)(2,1)}, bf16[128,1280]{1,0:T(8,128)(2,1)}, u32[]{:S(2)}, u32[]{:S(2)}) collective-permute-start(bf16[128,1280]{1,0:T(8,128)(2,1)} %pad_maximum_fusion.12), channel_id=1, source_target_pairs={{0,3},{1,2},{2,1},{3,0},{4,7},{5,6},{6,5},{7,4},{8,11},{9,10},{10,... | collective-permute-start | bytes 983048 | tf_op jit(solution)/shard_map/ppermute | solution.py:408
  16.4 15.4 %collective-permute-start = (bf16[128,1280]{1,0:T(8,128)(2,1)}, bf16[128,1280]{1,0:T(8,128)(2,1)}, u32[]{:S(2)}, u32[]{:S(2)}) collective-permute-start(bf16[128,1280]{1,0:T(8,128)(2,1)} %pad_maximum_fusion.10), channel_id=1, source_target_pairs={{0,1},{1,0},{2,3},{3,2},{4,5},{5,4},{6,7},{7,6},{8,9},{9,8},{10,11... | collective-permute-start | bytes 983048 | tf_op jit(solution)/shard_map/ppermute | solution.py:408
  16.7 3.1 collective-permute-start.3
  38.7 62.6 %all-to-all-start = ((bf16[4,272,2048]{2,1,0:T(8,128)(2,1)}), bf16[4,272,2048]{2,1,0:T(8,128)(2,1)}, u32[]{:S(2)}, u32[]{:S(2)}) async-start(bf16[4,272,2048]{2,1,0:T(8,128)(2,1)} %tile.8), calls=%async_computation | async-start | bytes 8912896 | tf_op jit(solution)/shard_map/all_to_all | solution.py:411
  44.1 1.7 collective-permute-start.7
  45.9 7.8 collective-permute-start.8
  48.0 37.5 %collective-permute-start.4 = (bf16[384,1280]{1,0:T(8,128)(2,1)}, bf16[384,1280]{1,0:T(8,128)(2,1)}, u32[]{:S(2)}, u32[]{:S(2)}) collective-permute-start(bf16[384,1280]{1,0:T(8,128)(2,1)} %constant_dynamic-update-slice_fusion.refs_0_), channel_id=1, source_target_pairs={{0,8},{1,9},{2,10},{3,11},{4,12},{5,13},{6,14},{7,15},{8,0},{9,1},... | collective-permute-start | bytes 2949128 | tf_op jit(solution)/shard_map/ppermute | solution.py:408
  54.5 26.6 %collective-permute-start.9 = (bf16[4,80,384]{1,2,0:T(8,128)(2,1)}, bf16[4,80,384]{1,2,0:T(8,128)(2,1)}, u32[]{:S(2)}, u32[]{:S(2)}) collective-permute-start(bf16[4,80,384]{1,2,0:T(8,128)(2,1)} %pad_maximum_fusion.9), channel_id=1, source_target_pairs={{0,16},{1,17},{2,18},{3,19},{4,20},{5,21},{6,22},{7,23},{8,24},{9,... | collective-permute-start | bytes 737288 | tf_op jit(solution)/shard_map/ppermute | solution.py:408
  59.0 37.3 %collective-permute-start.5 = (bf16[384,1280]{1,0:T(8,128)(2,1)}, bf16[384,1280]{1,0:T(8,128)(2,1)}, u32[]{:S(2)}, u32[]{:S(2)}) collective-permute-start(bf16[384,1280]{1,0:T(8,128)(2,1)} %constant_dynamic-update-slice_fusion.refs_0_), channel_id=1, source_target_pairs={{0,4},{1,5},{2,6},{3,7},{4,0},{5,1},{6,2},{7,3},{8,12},{9,13},{10,... | collective-permute-start | bytes 2949128 | tf_op jit(solution)/shard_map/ppermute | solution.py:408
  85.5 10.7 %collective-permute-start.6 = (bf16[384,1280]{1,0:T(8,128)(2,1)}, bf16[384,1280]{1,0:T(8,128)(2,1)S(1)}, u32[]{:S(2)}, u32[]{:S(2)}) collective-permute-start(bf16[384,1280]{1,0:T(8,128)(2,1)} %collective-permute-done.4.refs_1_), channel_id=1, source_target_pairs={{0,4},{1,5},{2,6},{3,7},{4,0},{5,1},{6,2},{7,3},{8,12},{9,13},{10,... | collective-permute-start | bytes 2949128 | tf_op jit(solution)/shard_map/ppermute | solution.py:408
  86.0 52.7 %copy-start.32 = (f32[8,640]{1,0:T(8,128)}, f32[8,640]{1,0:T(8,128)S(1)}, u32[]{:S(2)}) copy-start(f32[8,640]{1,0:T(8,128)S(1)} %pad_convert_fusion.w_ref) | copy-start | bytes 61444
  86.1 62.4 %copy-start.28 = (f32[8,640]{1,0:T(8,128)}, f32[8,640]{1,0:T(8,128)S(1)}, u32[]{:S(2)}) copy-start(f32[8,640]{1,0:T(8,128)S(1)} %select_maximum_fusion.soft_ref) | copy-start | bytes 61444
  111.2 74.9 %collective-permute-start.16 = (bf16[128,3072]{1,0:T(8,128)(2,1)}, bf16[128,3072]{1,0:T(8,128)(2,1)}, u32[]{:S(2)}, u32[]{:S(2)}) collective-permute-start(bf16[128,3072]{1,0:T(8,128)(2,1)} %pad_maximum_fusion.6), channel_id=1, source_target_pairs={{0,3},{1,2},{2,1},{3,0},{4,7},{5,6},{6,5},{7,4},{8,11},{9,10},{10,... | collective-permute-start | bytes 2359304 | tf_op jit(solution)/shard_map/ppermute | solution.py:408
  115.1 71.1 %collective-permute-start.15 = (bf16[128,3072]{1,0:T(8,128)(2,1)}, bf16[128,3072]{1,0:T(8,128)(2,1)}, u32[]{:S(2)}, u32[]{:S(2)}) collective-permute-start(bf16[128,3072]{1,0:T(8,128)(2,1)} %pad_maximum_fusion.5), channel_id=1, source_target_pairs={{0,2},{1,3},{2,0},{3,1},{4,6},{5,7},{6,4},{7,5},{8,10},{9,11},{10,... | collective-permute-start | bytes 2359304 | tf_op jit(solution)/shard_map/ppermute | solution.py:408
  117.8 20.7 %collective-permute-start.10 = (bf16[24,640]{1,0:T(8,128)(2,1)S(1)}, bf16[24,640]{1,0:T(8,128)(2,1)S(1)}, u32[]{:S(2)}, u32[]{:S(2)}) collective-permute-start(bf16[24,640]{1,0:T(8,128)(2,1)S(1)} %convolution_convert_fusion.10), channel_id=1, source_target_pairs={{0,4},{1,5},{2,6},{3,7},{4,8},{5,9},{6,10},{7,11},{8,12},{9,13},{1... | collective-permute-start | bytes 92168 | tf_op jit(solution)/shard_map/ppermute | solution.py:408
  122.2 73.3 %all-to-all-start.1 = ((bf16[4,256,2048]{2,1,0:T(8,128)(2,1)}), bf16[4,256,2048]{2,1,0:T(8,128)(2,1)}, u32[]{:S(2)}, u32[]{:S(2)}) async-start(bf16[4,256,2048]{2,1,0:T(8,128)(2,1)} %tile.9), calls=%async_computation.1 | async-start | bytes 8388608 | tf_op jit(solution)/shard_map/all_to_all | solution.py:411
  156.4 17.7 %collective-permute-start.11 = (f32[16,640]{1,0:T(8,128)S(1)}, f32[16,640]{1,0:T(8,128)S(1)}, u32[]{:S(2)}, u32[]{:S(2)}) collective-permute-start(f32[16,640]{1,0:T(8,128)S(1)} %get-tuple-element.140), channel_id=1, source_target_pairs={{0,4},{1,5},{2,6},{3,7},{4,8},{5,9},{6,10},{7,11},{8,12},{9,13},{1... | collective-permute-start | bytes 122888 | tf_op jit(solution)/shard_map/ppermute | solution.py:408
  161.7 12.5 %collective-permute-start.12 = (f32[16,640]{1,0:T(8,128)S(1)}, f32[16,640]{1,0:T(8,128)S(1)}, u32[]{:S(2)}, u32[]{:S(2)}) collective-permute-start(f32[16,640]{1,0:T(8,128)S(1)} %get-tuple-element.140), channel_id=1, source_target_pairs={{0,8},{1,9},{2,10},{3,11},{4,12},{5,13},{6,14},{7,15},{8,16},{9,17... | collective-permute-start | bytes 122888 | tf_op jit(solution)/shard_map/ppermute | solution.py:408
  164.1 8.2 %collective-permute-start.13 = (f32[8,640]{1,0:T(8,128)S(1)}, f32[8,640]{1,0:T(8,128)S(1)}, u32[]{:S(2)}, u32[]{:S(2)}) collective-permute-start(f32[8,640]{1,0:T(8,128)S(1)} %slice.348), channel_id=1, source_target_pairs={{4,0},{5,1},{6,2},{7,3},{8,4},{9,5},{10,6},{11,7},{12,8},{13,9},{1... | collective-permute-start | bytes 61448 | tf_op jit(solution)/shard_map/ppermute | solution.py:408
  172.3 23.2 %collective-permute-start.14 = (bf16[128,3072]{1,0:T(8,128)(2,1)S(1)}, bf16[128,3072]{1,0:T(8,128)(2,1)}, u32[]{:S(2)}, u32[]{:S(2)}) collective-permute-start(bf16[128,3072]{1,0:T(8,128)(2,1)S(1)} %copy-done.66), channel_id=1, source_target_pairs={{0,1},{1,0},{2,3},{3,2},{4,5},{5,4},{6,7},{7,6},{8,9},{9,8},{10,11... | collective-permute-start | bytes 2359304 | tf_op jit(solution)/shard_map/ppermute | solution.py:408
  195.5 65.2 %all-to-all-start.2 = ((bf16[4,256,2048]{2,1,0:T(8,128)(2,1)}), bf16[4,256,2048]{2,1,0:T(8,128)(2,1)}, u32[]{:S(2)}, u32[]{:S(2)}) async-start(bf16[4,256,2048]{2,1,0:T(8,128)(2,1)} %bitcast.182), calls=%async_computation.2 | async-start | bytes 8388608 | tf_op jit(solution)/shard_map/all_to_all | solution.py:411
  205.6 55.2 %collective-permute-start.17 = (bf16[384,3072]{1,0:T(8,128)(2,1)S(1)}, bf16[384,3072]{1,0:T(8,128)(2,1)}, u32[]{:S(2)}, u32[]{:S(2)}) collective-permute-start(bf16[384,3072]{1,0:T(8,128)(2,1)S(1)} %constant_dynamic-update-slice_fusion.3.refs_0_), channel_id=1, source_target_pairs={{0,8},{1,9},{2,10},{3,11},{4,12},{5,13},{6,14},{7,15},{8,0},{9,1},... | collective-permute-start | bytes 7077896 | tf_op jit(solution)/shard_map/ppermute | solution.py:408
  268.2 51.9 %all-to-all-start.3 = ((bf16[4,256,2048]{2,1,0:T(8,128)(2,1)}), bf16[4,256,2048]{2,1,0:T(8,128)(2,1)}, u32[]{:S(2)}, u32[]{:S(2)}) async-start(bf16[4,256,2048]{2,1,0:T(8,128)(2,1)} %tile.10), calls=%async_computation.3 | async-start | bytes 8388608 | tf_op jit(solution)/shard_map/all_to_all | solution.py:411
  273.1 4.9 collective-permute-start.18
  273.2 8.2 %collective-permute-start.19 = (bf16[384,3072]{1,0:T(8,128)(2,1)}, bf16[384,3072]{1,0:T(8,128)(2,1)}, u32[]{:S(2)}, u32[]{:S(2)}) collective-permute-start(bf16[384,3072]{1,0:T(8,128)(2,1)} %collective-permute-done.17.refs_1_), channel_id=1, source_target_pairs={{0,4},{1,5},{2,6},{3,7},{4,0},{5,1},{6,2},{7,3},{8,12},{9,13},{10,... | collective-permute-start | bytes 7077896 | tf_op jit(solution)/shard_map/ppermute | solution.py:408
  349.7 21.4 %collective-permute-start.20 = (bf16[768,2048]{1,0:T(8,128)(2,1)}, bf16[768,2048]{1,0:T(8,128)(2,1)S(1)}, u32[]{:S(2)}, u32[]{:S(2)}) collective-permute-start(bf16[768,2048]{1,0:T(8,128)(2,1)} %convolution_convert_fusion.8), channel_id=1, source_target_pairs={{0,4},{1,5},{2,6},{3,7},{4,0},{5,1},{6,2},{7,3},{8,12},{9,13},{10,... | collective-permute-start | bytes 9437192 | tf_op jit(solution)/shard_map/ppermute | solution.py:408
  374.2 41.6 %all-to-all-start.4 = ((bf16[4,192,2048]{2,1,0:T(8,128)(2,1)}), bf16[4,192,2048]{2,1,0:T(8,128)(2,1)}, u32[]{:S(2)}, u32[]{:S(2)}) async-start(bf16[4,192,2048]{2,1,0:T(8,128)(2,1)} %bitcast.177), calls=%async_computation.4 | async-start | bytes 6291456 | tf_op jit(solution)/shard_map/all_to_all | solution.py:411
  417.9 52.3 %all-to-all-start.5 = ((bf16[4,256,2048]{2,1,0:T(8,128)(2,1)}), bf16[4,256,2048]{2,1,0:T(8,128)(2,1)}, u32[]{:S(2)}, u32[]{:S(2)}) async-start(bf16[4,256,2048]{2,1,0:T(8,128)(2,1)} %bitcast.181), calls=%async_computation.5 | async-start | bytes 8388608 | tf_op jit(solution)/shard_map/all_to_all | solution.py:411
  422.8 326.9 %reduce-scatter.5.cloned.1.call-start = ((), (), s32[]{:S(2)}) async-start(), calls=%async_computation.14 | async-start | bytes 14155776 | tf_op jit(solution)/shard_map/reduce_scatter | solution.py:645
  422.9 21.3 %collective-permute-start.21 = (bf16[192,2048]{1,0:T(8,128)(2,1)}, bf16[192,2048]{1,0:T(8,128)(2,1)}, u32[]{:S(2)}, u32[]{:S(2)}) collective-permute-start(bf16[192,2048]{1,0:T(8,128)(2,1)} %constant_dynamic-slice_fusion.13), channel_id=1, source_target_pairs={{0,8},{1,9},{2,10},{3,11},{4,12},{5,13},{6,14},{7,15},{8,16},{9,17... | collective-permute-start | bytes 2359304 | tf_op jit(solution)/shard_map/ppermute | solution.py:408
  482.1 50.9 %all-to-all-start.6 = ((bf16[4,256,2048]{2,1,0:T(8,128)(2,1)}), bf16[4,256,2048]{2,1,0:T(8,128)(2,1)}, u32[]{:S(2)}, u32[]{:S(2)}) async-start(bf16[4,256,2048]{2,1,0:T(8,128)(2,1)} %tile.11), calls=%async_computation.6 | async-start | bytes 8388608 | tf_op jit(solution)/shard_map/all_to_all | solution.py:411
  487.1 38.4 %collective-permute-start.22 = (bf16[192,2048]{1,0:T(8,128)(2,1)}, bf16[192,2048]{1,0:T(8,128)(2,1)S(1)}, u32[]{:S(2)}, u32[]{:S(2)}) collective-permute-start(bf16[192,2048]{1,0:T(8,128)(2,1)} %convert_add_fusion.4), channel_id=1, source_target_pairs={{0,8},{1,9},{2,10},{3,11},{4,12},{5,13},{6,14},{7,15},{8,16},{9,17... | collective-permute-start | bytes 2359304 | tf_op jit(solution)/shard_map/ppermute | solution.py:408
  533.1 70.1 %all-to-all-start.7 = ((bf16[4,256,2048]{2,1,0:T(8,128)(2,1)}), bf16[4,256,2048]{2,1,0:T(8,128)(2,1)}, u32[]{:S(2)}, u32[]{:S(2)}) async-start(bf16[4,256,2048]{2,1,0:T(8,128)(2,1)} %bitcast.179), calls=%async_computation.7 | async-start | bytes 8388608 | tf_op jit(solution)/shard_map/all_to_all | solution.py:411
  556.6 7.1 collective-permute-start.23
  558.0 6.9 collective-permute-start.24
  560.9 39.8 %collective-permute-start.26 = (bf16[192,2048]{1,0:T(8,128)(2,1)}, bf16[192,2048]{1,0:T(8,128)(2,1)S(1)}, u32[]{:S(2)}, u32[]{:S(2)}) collective-permute-start(bf16[192,2048]{1,0:T(8,128)(2,1)} %convert_add_fusion.3), channel_id=1, source_target_pairs={{0,8},{1,9},{2,10},{3,11},{4,12},{5,13},{6,14},{7,15},{8,16},{9,17... | collective-permute-start | bytes 2359304 | tf_op jit(solution)/shard_map/ppermute | solution.py:408
  583.9 3.1 collective-permute-start.25
  623.6 13.7 %collective-permute-start.27 = (bf16[1024,1280]{1,0:T(8,128)(2,1)}, bf16[1024,1280]{1,0:T(8,128)(2,1)}, u32[]{:S(2)}, u32[]{:S(2)}) collective-permute-start(bf16[1024,1280]{1,0:T(8,128)(2,1)} %convolution_convert_fusion.6), channel_id=1, source_target_pairs={{0,4},{1,5},{2,6},{3,7},{4,0},{5,1},{6,2},{7,3},{8,12},{9,13},{10,... | collective-permute-start | bytes 7864328 | tf_op jit(solution)/shard_map/ppermute | solution.py:408
  639.1 18.7 %collective-permute-start.28 = (bf16[256,1280]{1,0:T(8,128)(2,1)S(1)}, bf16[256,1280]{1,0:T(8,128)(2,1)S(1)}, u32[]{:S(2)}, u32[]{:S(2)}) collective-permute-start(bf16[256,1280]{1,0:T(8,128)(2,1)S(1)} %add_convert_fusion.4), channel_id=1, source_target_pairs={{0,8},{1,9},{2,10},{3,11},{4,12},{5,13},{6,14},{7,15},{8,16},{9,17... | collective-permute-start | bytes 1966088 | tf_op jit(solution)/shard_map/ppermute | solution.py:408
  660.0 72.3 %all-to-all-start.8 = ((bf16[4,256,2048]{2,1,0:T(8,128)(2,1)}), bf16[4,256,2048]{2,1,0:T(8,128)(2,1)}, u32[]{:S(2)}, u32[]{:S(2)}) async-start(bf16[4,256,2048]{2,1,0:T(8,128)(2,1)} %bitcast.180), calls=%async_computation.8 | async-start | bytes 8388608 | tf_op jit(solution)/shard_map/all_to_all | solution.py:411
  664.8 98.8 %reduce-scatter.3.cloned.1.call-start = ((), (), s32[]{:S(2)}) async-start(), calls=%async_computation.13 | async-start | bytes 3502080 | tf_op jit(solution)/shard_map/reduce_scatter | solution.py:718
  673.0 21.9 %collective-permute-start.29 = (bf16[256,1280]{1,0:T(8,128)(2,1)}, bf16[256,1280]{1,0:T(8,128)(2,1)}, u32[]{:S(2)}, u32[]{:S(2)}) collective-permute-start(bf16[256,1280]{1,0:T(8,128)(2,1)} %add_add_fusion.3), channel_id=1, source_target_pairs={{0,8},{1,9},{2,10},{3,11},{4,12},{5,13},{6,14},{7,15},{8,16},{9,17... | collective-permute-start | bytes 1966088 | tf_op jit(solution)/shard_map/ppermute | solution.py:408
  697.4 32.0 %collective-permute-start.30 = (bf16[256,1280]{1,0:T(8,128)(2,1)}, bf16[256,1280]{1,0:T(8,128)(2,1)}, u32[]{:S(2)}, u32[]{:S(2)}) collective-permute-start(bf16[256,1280]{1,0:T(8,128)(2,1)} %add_convert_fusion.3), channel_id=1, source_target_pairs={{0,8},{1,9},{2,10},{3,11},{4,12},{5,13},{6,14},{7,15},{8,16},{9,17... | collective-permute-start | bytes 1966088 | tf_op jit(solution)/shard_map/ppermute | solution.py:408
  736.4 21.2 %all-to-all-start.9 = ((bf16[4,64,1408]{2,1,0:T(8,128)(2,1)}), bf16[4,64,1408]{2,1,0:T(8,128)(2,1)S(1)}, u32[]{:S(2)}, u32[]{:S(2)}) async-start(bf16[4,64,1408]{2,1,0:T(8,128)(2,1)} %bitcast.184), calls=%async_computation.9 | async-start | bytes 1441792 | tf_op jit(solution)/shard_map/all_to_all | solution.py:411
  757.6 34.2 %all-to-all-start.10 = ((bf16[4,64,3200]{2,1,0:T(8,128)(2,1)}), bf16[4,64,3200]{2,1,0:T(8,128)(2,1)}, u32[]{:S(2)}, u32[]{:S(2)}) async-start(bf16[4,64,3200]{2,1,0:T(8,128)(2,1)} %bitcast.178), calls=%async_computation.12 | async-start | bytes 3276800 | tf_op jit(solution)/shard_map/all_to_all | solution.py:411
  763.6 4.9 collective-permute-start.31
  (87 other events, 635.3 us)
Sparse Core Ops, SparseCore 0:
  470.3 162.3 reduce-scatter.4
  677.0 58.5 reduce-scatter.2
